TPU v7x, 256 devices: a whole 4x4x8 slice. The times are simulated.
256 devices in a mesh: sector: 16 (over y_hi, z), radial: 16 (over x, y_lo, core).
Axes of the slice: x: 4, y: 4 (y_hi: 2, y_lo: 2; y = y_hi * 2 + y_lo), z: 8, core: 2. Of those that a mesh axis runs over, the one named last changes fastest.
Arguments:
- density: float32 [2048, 256, 128], P('sector', 'radial'), may hold values from 0.4 to 1.2
- swirl: float32 [2048, 256, 128], P('sector', 'radial'), may hold values from -4 to 4
- heat_rate: float32 [2048, 256, 128], P('sector', 'radial'), may hold values from 0.1 to 3
- acoustic: float32 [3, 2048, 128], P(None, 'sector'), may hold values from -5 to 5
- mode_impedance: float32 [1025], replicated, may hold values from 0.05 to 8
- mouth_azimuth: int32 [16], replicated, may hold values from 0 to 120, as said below
- mouth_radius: int32 [16], replicated, may hold values from 0 to 248, as said below
Outputs:
- density_next: float32 [2048, 256, 128], P('sector', 'radial')
- pressure: float32 [2048, 256, 128], P('sector', 'radial')
- acoustic_next: float32 [3, 2048, 128], P(None, 'sector')
Inputs may be any that keep to these rules, and one draw needn't show every extreme that they name: Burner b's mouth starts at azimuthal cell b * 128 + mouth_azimuth[b] and spans 8 cells. Burner b's mouth spans radial cells mouth_radius[b] to mouth_radius[b] + 7.
All inputs are finite; a program needn't handle non-finite values.
Results may differ from a plain program's by a relative error of at most 0.00018.
Values sent between devices are 32-bit elements; how exact they have to be, the bound alone decides.
A program may use at most 128 MiB of HBM per device.

v0:
```python
import math

import jax
import jax.numpy as jnp
from jax import lax
from jax.sharding import PartitionSpec as P

BURNERS = 16
MOUTH = 8
SWEEPS = 4
SUBSTEPS = 8


time_step = 0.2
diffusion = 0.05
inflow_rate = 0.5
wave_speed = 0.5
heat_coupling = 0.5
feedback = 0.5


def from_everyone(x, axis):
    count = lax.axis_size(axis)
    return lax.all_to_all(jnp.broadcast_to(x[None], (count, *x.shape)), axis, 0, 0, tiled=True)


def over_copies(x, axis):
    everything = from_everyone(x, axis)
    return jnp.sum(everything, axis=0)


def passed_along(value, axis, steps):
    count = lax.axis_size(axis)
    pairs = [(source, (source + steps) % count) for source in range(count)]
    return lax.ppermute(value, axis, pairs)


def padded(cells, sides, width, closed):
    for axis, dim in sides:
        count = lax.axis_size(axis)
        ends = count if closed else count - 1
        head = lax.slice_in_dim(cells, 0, width, axis=dim)
        tail = lax.slice_in_dim(cells, cells.shape[dim] - width, cells.shape[dim], axis=dim)
        cells = jnp.concatenate(
            [
                lax.ppermute(tail, axis, [(i, (i + 1) % count) for i in range(ends)]),
                cells,
                lax.ppermute(head, axis, [((i + 1) % count, i) for i in range(ends)]),
            ],
            axis=dim,
        )
    return cells


def axial_pair(field):
    zeros = jnp.zeros_like(field[:, :, :1])
    return jnp.concatenate([field[:, :, 1:], zeros], 2) + jnp.concatenate(
        [zeros, field[:, :, :-1]], 2
    )


def radial_pair(field):
    zeros = jnp.zeros_like(field[:, :1])
    return jnp.concatenate([field[:, 1:], zeros], 1) + jnp.concatenate([zeros, field[:, :-1]], 1)


def mode_order(mode_rows, n_theta):
    half = n_theta // 2
    return jnp.where(mode_rows <= half, mode_rows, mode_rows - half)


def spectral_basis(mode_rows, theta_cols, n_theta):
    half = n_theta // 2
    order = mode_order(mode_rows, n_theta)
    phase = order[:, None] * theta_cols[None, :] % n_theta
    angle = phase.astype(jnp.float32) * (2.0 * math.pi / n_theta)
    return jnp.where((mode_rows <= half)[:, None], jnp.cos(angle), jnp.sin(angle))


def inverse_weight(mode_rows, n_theta):
    half = n_theta // 2
    edge = (mode_rows == 0) | (mode_rows == half)
    return jnp.where(edge, 1.0, 2.0).astype(jnp.float32) / n_theta


def row_blocks(n_theta):
    count = max(n_theta // 512, 1)
    return (count, n_theta // count)


def forward_transform(columns):
    n_theta = columns.shape[0]
    count, size = row_blocks(n_theta)
    theta_cols = jnp.arange(n_theta, dtype=jnp.int32)

    def forward_one_block(block):
        mode_rows = block * size + jnp.arange(size, dtype=jnp.int32)
        basis = spectral_basis(mode_rows, theta_cols, n_theta)
        return jnp.dot(
            basis, columns, precision=lax.Precision.HIGHEST, preferred_element_type=jnp.float32
        )

    result = lax.map(forward_one_block, jnp.arange(count, dtype=jnp.int32))
    return result.reshape(n_theta, columns.shape[1])


def inverse_transform(columns):
    n_theta = columns.shape[0]
    count, size = row_blocks(n_theta)
    mode_rows = jnp.arange(n_theta, dtype=jnp.int32)
    weighted = columns * inverse_weight(mode_rows, n_theta)[:, None]

    def inverse_one_block(block):
        theta_cols = block * size + jnp.arange(size, dtype=jnp.int32)
        basis = spectral_basis(mode_rows, theta_cols, n_theta)
        return lax.dot_general(
            basis,
            weighted,
            (((0,), (0,)), ((), ())),
            precision=lax.Precision.HIGHEST,
            preferred_element_type=jnp.float32,
        )

    result = lax.map(inverse_one_block, jnp.arange(count, dtype=jnp.int32))
    return result.reshape(n_theta, columns.shape[1])


def forward_lines(items):
    shape = items.shape
    flat = items.reshape(shape[0], shape[1] * shape[2] * shape[3])
    return forward_transform(flat).reshape(shape)


def advance(wave_press, wave_along, wave_axial, source, fetch_above, fetch_below):
    zeros = jnp.zeros_like(wave_press[:, :1])
    for substep in range(SUBSTEPS):
        above = fetch_above(wave_press[:1])
        press_up = jnp.concatenate([wave_press[1:], above], 0)
        press_axial = jnp.concatenate([wave_press[:, 1:], zeros], 1)
        wave_along = wave_along - wave_speed * (press_up - wave_press)
        wave_axial = wave_axial - wave_speed * (press_axial - wave_press)
        below = fetch_below(wave_along[-1:])
        along_down = jnp.concatenate([below, wave_along[:-1]], 0)
        axial_down = jnp.concatenate([zeros, wave_axial[:, :-1]], 1)
        wave_press = (
            wave_press
            - wave_speed * (wave_along - along_down + (wave_axial - axial_down))
            + heat_coupling * source
        )
    return jnp.stack([wave_press, wave_along, wave_axial])


def shards(density, swirl, heat_rate, acoustic, mode_impedance, mouth_azimuth, mouth_radius):
    sectors = lax.axis_size("sector")
    radials = lax.axis_size("radial")
    cells_theta, cells_radius, cells_axial = density.shape
    n_theta = cells_theta * sectors
    n_radius = cells_radius * radials
    sector_index = lax.axis_index("sector")
    radial_index = lax.axis_index("radial")
    theta_global = sector_index * cells_theta + jnp.arange(cells_theta, dtype=jnp.int32)
    radius_global = radial_index * cells_radius + jnp.arange(cells_radius, dtype=jnp.int32)
    theta_start = jnp.arange(BURNERS, dtype=jnp.int32) * (n_theta // BURNERS) + mouth_azimuth
    inside_theta = (
        (theta_global[None, :] >= theta_start[:, None])
        & (theta_global[None, :] < theta_start[:, None] + MOUTH)
    ).astype(jnp.float32)
    inside_radius = (
        (radius_global[None, :] >= mouth_radius[:, None])
        & (radius_global[None, :] < mouth_radius[:, None] + MOUTH)
    ).astype(jnp.float32)
    mouth_mask = lax.dot_general(
        inside_theta, inside_radius, (((0,), (0,)), ((), ())), preferred_element_type=jnp.float32
    )
    heat_field = heat_rate * density * density
    local_heat = jnp.sum(heat_field, axis=1) / n_radius
    source = over_copies(local_heat, "radial")

    def fetch_above(row):
        return passed_along(row, "sector", -1)

    def fetch_below(row):
        return passed_along(row, "sector", 1)

    acoustic_next = advance(acoustic[0], acoustic[1], acoustic[2], source, fetch_above, fetch_below)
    swirl_flux = swirl * density
    azimuth_ext = padded(jnp.stack([density, swirl_flux]), (("sector", 1),), 1, True)
    radial_ext = padded(density, (("radial", 1),), 1, False)
    twice = 2.0 * density
    laplace = (
        azimuth_ext[0, 2:]
        + azimuth_ext[0, :-2]
        - twice
        + (radial_ext[:, 2:] + radial_ext[:, :-2] - twice)
        + (axial_pair(density) - twice)
    )
    advection = -0.5 * (azimuth_ext[1, 2:] - azimuth_ext[1, :-2])
    density_next = (
        density
        + time_step * (advection + diffusion * laplace)
        + inflow_rate * mouth_mask[:, :, None] * (1.0 - density)
    )
    forcing = (density_next - density) / time_step + feedback * acoustic_next[0][:, None, :]
    axial_block = cells_axial // sectors
    reach = SWEEPS - 1
    half = n_theta // 2
    lines = forward_lines(
        lax.all_to_all(
            forcing.reshape(cells_theta, cells_radius, sectors, axial_block),
            "sector",
            split_axis=2,
            concat_axis=0,
            tiled=True,
        )
    )
    lines = lines.reshape(n_theta, cells_radius, axial_block)
    all_rows = jnp.arange(n_theta, dtype=jnp.int32)
    all_order = mode_order(all_rows, n_theta)
    impedance_all = jnp.concatenate([mode_impedance, mode_impedance[1:half]], 0)
    shifted_all = 2.0 - 2.0 * jnp.cos(all_order.astype(jnp.float32) * (2.0 * math.pi / n_theta))
    diagonal_all = (4.0 + shifted_all + impedance_all)[:, None, None]
    lines_ext = padded(lines, (("sector", 2), ("radial", 1)), reach, False)
    radius_ext = (
        radial_index * cells_radius - reach + jnp.arange(cells_radius + 2 * reach, dtype=jnp.int32)
    )
    axial_ext = (
        sector_index * axial_block - reach + jnp.arange(axial_block + 2 * reach, dtype=jnp.int32)
    )
    valid_radius = ((radius_ext >= 0) & (radius_ext < n_radius)).astype(jnp.float32)
    valid_axial = ((axial_ext >= 0) & (axial_ext < cells_axial)).astype(jnp.float32)
    valid = (valid_radius[:, None] * valid_axial[None, :])[None]
    solution = lines_ext / diagonal_all * valid
    for sweep in range(SWEEPS - 1):
        solution = (lines_ext + radial_pair(solution) + axial_pair(solution)) / diagonal_all * valid
    solution = solution[:, reach : reach + cells_radius, reach : reach + axial_block]
    pressure_lines = inverse_transform(solution.reshape(n_theta, cells_radius * axial_block))
    pressure_lines = pressure_lines.reshape(n_theta, cells_radius, 1, axial_block)
    pressure = lax.all_to_all(
        pressure_lines, "sector", split_axis=0, concat_axis=2, tiled=True
    ).reshape(cells_theta, cells_radius, cells_axial)
    return (density_next, pressure, acoustic_next)


def solution(mesh):
    return jax.shard_map(
        shards,
        mesh=mesh,
        in_specs=(
            P("sector", "radial", None),
            P("sector", "radial", None),
            P("sector", "radial", None),
            P(None, "sector", None),
            P(),
            P(),
            P(),
        ),
        out_specs=(
            P("sector", "radial", None),
            P("sector", "radial", None),
            P(None, "sector", None),
        ),
        check_vma=False,
    )
```

profile of v0, /device:TPU:10, one launch (start us, length us, event | category | flops | bytes accessed | tf_op | source)
XLA Modules:
  0.0 489.0 jit_solution(17043962884829477089)
XLA Ops:
  3.6 5.7 %all-to-all-start = ((f32[16,128,128]{2,1,0:T(8,128)}), f32[16,128,128]{2,1,0:T(8,128)S(1)}, u32[]{:S(2)}, u32[]{:S(2)}) async-start(f32[16,128,128]{2,1,0:T(8,128)} %broadcast_in_dim.71), calls=%async_computation | async-start | bytes 2097152 | tf_op jit(solution)/shard_map/all_to_all | solution.py:24
  9.4 7.7 %collective-permute-start.4 = (f32[1,128]{1,0:T(1,128)S(1)}, f32[1,128]{1,0:T(1,128)S(1)}, u32[]{:S(2)}, u32[]{:S(2)}) collective-permute-start(f32[1,128]{1,0:T(1,128)S(1)} %slice_bitcast_fusion.2), channel_id=1, source_target_pairs={{0,240},{16,0},{32,16},{48,32},{64,48},{80,64},{96,80},{112,96},{1... | collective-permute-start | bytes 1544 | tf_op jit(solution)/shard_map/ppermute | solution.py:35
  18.5 4.3 all-to-all-done
  26.0 4.6 collective-permute-start.6
  32.0 7.4 %collective-permute-done.7 = f32[1,128]{1,0:T(1,128)S(1)} collective-permute-done((f32[1,128]{1,0:T(1,128)S(1)}, f32[1,128]{1,0:T(1,128)S(1)}, u32[]{:S(2)}, u32[]{:S(2)}) %collective-permute-start.7) | collective-permute-done | bytes 544 | tf_op jit(solution)/shard_map/ppermute | solution.py:35
  43.2 7.1 %collective-permute-done.9 = f32[1,128]{1,0:T(1,128)S(1)} collective-permute-done((f32[1,128]{1,0:T(1,128)S(1)}, f32[1,128]{1,0:T(1,128)S(1)}, u32[]{:S(2)}, u32[]{:S(2)}) %collective-permute-start.9) | collective-permute-done | bytes 544 | tf_op jit(solution)/shard_map/ppermute | solution.py:35
  56.3 5.1 %collective-permute-done.11 = f32[1,128]{1,0:T(1,128)S(1)} collective-permute-done((f32[1,128]{1,0:T(1,128)S(1)}, f32[1,128]{1,0:T(1,128)S(1)}, u32[]{:S(2)}, u32[]{:S(2)}) %collective-permute-start.11) | collective-permute-done | bytes 544 | tf_op jit(solution)/shard_map/ppermute | solution.py:35
  70.2 5.7 %collective-permute-start = (f32[2,1,16,128]{3,2,1,0:T(8,128)S(1)}, f32[2,1,16,128]{3,2,1,0:T(8,128)S(1)}, u32[]{:S(2)}, u32[]{:S(2)}) collective-permute-start(f32[2,1,16,128]{3,2,1,0:T(8,128)S(1)} %copy.94), channel_id=1, source_target_pairs={{16,0},{32,16},{48,32},{64,48},{80,64},{96,80},{112,96},{128,112},... | collective-permute-start | bytes 49160 | tf_op jit(solution)/shard_map/ppermute | solution.py:48
  78.4 5.7 %collective-permute-start.14 = (f32[1,128]{1,0:T(1,128)S(1)}, f32[1,128]{1,0:T(1,128)S(1)}, u32[]{:S(2)}, u32[]{:S(2)}) collective-permute-start(f32[1,128]{1,0:T(1,128)S(1)} %slice.375), channel_id=1, source_target_pairs={{0,240},{16,0},{32,16},{48,32},{64,48},{80,64},{96,80},{112,96},{1... | collective-permute-start | bytes 1544 | tf_op jit(solution)/shard_map/ppermute | solution.py:35
  90.2 5.7 %collective-permute-done.15 = f32[1,128]{1,0:T(1,128)S(1)} collective-permute-done((f32[1,128]{1,0:T(1,128)S(1)}, f32[1,128]{1,0:T(1,128)S(1)}, u32[]{:S(2)}, u32[]{:S(2)}) %collective-permute-start.15) | collective-permute-done | bytes 544 | tf_op jit(solution)/shard_map/ppermute | solution.py:35
  99.8 7.1 %collective-permute-done.17 = f32[1,128]{1,0:T(1,128)S(1)} collective-permute-done((f32[1,128]{1,0:T(1,128)S(1)}, f32[1,128]{1,0:T(1,128)S(1)}, u32[]{:S(2)}, u32[]{:S(2)}) %collective-permute-start.17) | collective-permute-done | bytes 544 | tf_op jit(solution)/shard_map/ppermute | solution.py:35
  123.6 4.1 all-to-all-start.1
  127.7 26.6 %all-to-all-done.1 = f32[128,16,16,8]{0,3,1,2:T(8,128)S(1)} async-done(((f32[128,16,16,8]{0,3,1,2:T(8,128)}), f32[128,16,16,8]{0,3,1,2:T(8,128)S(1)}, u32[]{:S(2)}, u32[]{:S(2)}) %all-to-all-start.1) | async-done | bytes 1048608 | tf_op jit(solution)/shard_map/all_to_all | solution.py:208
  156.8 103.1 %while.27 = (s32[]{:T(128)}, f32[4,512,128]{1,0,2:T(4,128)S(1)}, s32[4]{0:T(128)S(1)}, f32[2048,128]{1,0:T(8,128)}, s32[]{:T(128)}, /*index=5*/s32[1]{0:T(128)}, s32[]{:T(128)}) while((s32[]{:T(128)}, f32[4,512,128]{1,0,2:T(4,128)S(1)}, s32[4]{0:T(128)S(1)}, f32[2048,128]{1,0:T(8,128)}, s32[]{:T(128)}, /*index=5*/s32[1]{0:T(128)}, ...), condition=%wide.region_3.4_spmd.clone, body=%wide.region_2.3_spmd.clone.sunk | while | flops 1626344448 | bytes 2364529 | solution.py:103
  158.3 21.8 %fusion.165 = f32[1,512,128]{2,1,0:T(8,128)S(1)} fusion(f32[2048,128]{1,0:T(8,128)} %get-tuple-element.353, s32[512]{0:T(512)S(1)} %add_select_fusion.4, pred[512]{0:T(512)(128)(4,1)S(1)} %fusion.164), kind=kOutput, calls=%fused_computation.22.clone.1 | convolution fusion | flops 1626341376 | bytes 1313280 | tf_op jit(solution)/shard_map/while/body/eval_jaxpr/dot_general | solution.py:99
  184.0 21.8 %fusion.165 = f32[1,512,128]{2,1,0:T(8,128)S(1)} fusion(f32[2048,128]{1,0:T(8,128)} %get-tuple-element.353, s32[512]{0:T(512)S(1)} %add_select_fusion.4, pred[512]{0:T(512)(128)(4,1)S(1)} %fusion.164), kind=kOutput, calls=%fused_computation.22.clone.1 | convolution fusion | flops 1626341376 | bytes 1313280 | tf_op jit(solution)/shard_map/while/body/eval_jaxpr/dot_general | solution.py:99
  209.7 21.8 %fusion.165 = f32[1,512,128]{2,1,0:T(8,128)S(1)} fusion(f32[2048,128]{1,0:T(8,128)} %get-tuple-element.353, s32[512]{0:T(512)S(1)} %add_select_fusion.4, pred[512]{0:T(512)(128)(4,1)S(1)} %fusion.164), kind=kOutput, calls=%fused_computation.22.clone.1 | convolution fusion | flops 1626341376 | bytes 1313280 | tf_op jit(solution)/shard_map/while/body/eval_jaxpr/dot_general | solution.py:99
  235.5 21.8 %fusion.165 = f32[1,512,128]{2,1,0:T(8,128)S(1)} fusion(f32[2048,128]{1,0:T(8,128)} %get-tuple-element.353, s32[512]{0:T(512)S(1)} %add_select_fusion.4, pred[512]{0:T(512)(128)(4,1)S(1)} %fusion.164), kind=kOutput, calls=%fused_computation.22.clone.1 | convolution fusion | flops 1626341376 | bytes 1313280 | tf_op jit(solution)/shard_map/while/body/eval_jaxpr/dot_general | solution.py:99
  266.3 6.7 %collective-permute-done.20 = f32[2048,16,3]{0,2,1:T(4,128)S(1)} collective-permute-done((f32[2048,16,3]{0,2,1:T(4,128)}, f32[2048,16,3]{0,2,1:T(4,128)S(1)}, u32[]{:S(2)}, u32[]{:S(2)}) %collective-permute-start.20) | collective-permute-done | bytes 393248 | tf_op jit(solution)/shard_map/ppermute | solution.py:46
  273.0 4.0 collective-permute-done.21
  284.0 7.6 %collective-permute-done.22 = f32[2048,3,14]{0,2,1:T(8,128)S(1)} collective-permute-done((f32[2048,3,14]{0,2,1:T(8,128)}, f32[2048,3,14]{0,2,1:T(8,128)S(1)}, u32[]{:S(2)}, u32[]{:S(2)}) %collective-permute-start.22) | collective-permute-done | bytes 344096 | tf_op jit(solution)/shard_map/ppermute | solution.py:46
  306.2 119.2 %while.28 = (s32[]{:T(128)}, f32[4,512,128]{1,0,2:T(4,128)S(1)}, s32[4]{0:T(128)S(1)}, f32[2048,128]{1,0:T(8,128)}, s32[]{:T(128)}, /*index=5*/s32[1]{0:T(128)}, s32[]{:T(128)}) while((s32[]{:T(128)}, f32[4,512,128]{1,0,2:T(4,128)S(1)}, s32[4]{0:T(128)S(1)}, f32[2048,128]{1,0:T(8,128)}, s32[]{:T(128)}, ...), condition=%wide.region_5.6_spmd.clone.clone, body=%wide.region_4.5_spmd.clone.clone.sunk | while | flops 1626350080 | bytes 2383981 | solution.py:124
  307.5 25.9 %fusion.168 = f32[1,512,128]{2,1,0:T(8,128)S(1)} fusion(f32[2048,128]{1,0:T(8,128)} %get-tuple-element.374, s32[512]{0:T(512)S(1)} %iota_add_fusion.6, s32[2048]{0:T(1024)S(1)} %iota_select_fusion.2, pred[2048]{0:T(1024)(128)(4,1)S(1)} %iota_compare_fusion.4), kind=kOutput, calls=%fused_computation.52.clone.1 | convolution fusion | flops 1626341376 | bytes 1323008 | tf_op jit(solution)/shard_map/while/body/eval_jaxpr/dot_general | solution.py:116
  337.2 25.9 %fusion.168 = f32[1,512,128]{2,1,0:T(8,128)S(1)} fusion(f32[2048,128]{1,0:T(8,128)} %get-tuple-element.374, s32[512]{0:T(512)S(1)} %iota_add_fusion.6, s32[2048]{0:T(1024)S(1)} %iota_select_fusion.2, pred[2048]{0:T(1024)(128)(4,1)S(1)} %iota_compare_fusion.4), kind=kOutput, calls=%fused_computation.52.clone.1 | convolution fusion | flops 1626341376 | bytes 1323008 | tf_op jit(solution)/shard_map/while/body/eval_jaxpr/dot_general | solution.py:116
  367.0 25.9 %fusion.168 = f32[1,512,128]{2,1,0:T(8,128)S(1)} fusion(f32[2048,128]{1,0:T(8,128)} %get-tuple-element.374, s32[512]{0:T(512)S(1)} %iota_add_fusion.6, s32[2048]{0:T(1024)S(1)} %iota_select_fusion.2, pred[2048]{0:T(1024)(128)(4,1)S(1)} %iota_compare_fusion.4), kind=kOutput, calls=%fused_computation.52.clone.1 | convolution fusion | flops 1626341376 | bytes 1323008 | tf_op jit(solution)/shard_map/while/body/eval_jaxpr/dot_general | solution.py:116
  396.8 25.9 %fusion.168 = f32[1,512,128]{2,1,0:T(8,128)S(1)} fusion(f32[2048,128]{1,0:T(8,128)} %get-tuple-element.374, s32[512]{0:T(512)S(1)} %iota_add_fusion.6, s32[2048]{0:T(1024)S(1)} %iota_select_fusion.2, pred[2048]{0:T(1024)(128)(4,1)S(1)} %iota_compare_fusion.4), kind=kOutput, calls=%fused_computation.52.clone.1 | convolution fusion | flops 1626341376 | bytes 1323008 | tf_op jit(solution)/shard_map/while/body/eval_jaxpr/dot_general | solution.py:116
  426.1 4.8 copy.115
  430.9 7.1 %reshape.158 = f32[16,1,16384]{2,1,0:T(1,128)} reshape(f32[2048,1,8,16]{3,2,1,0:T(8,128)} %bitcast.102) | data formatting | bytes 2097152
  438.0 6.8 %all-to-all-start.2 = ((f32[16,1,16384]{2,1,0:T(1,128)}), f32[16,1,16384]{2,1,0:T(1,128)S(1)}, u32[]{:S(2)}, u32[]{:S(2)}) async-start(f32[16,1,16384]{2,1,0:T(1,128)} %reshape.158), calls=%async_computation.2 | async-start | bytes 2097152 | tf_op jit(solution)/shard_map/all_to_all | solution.py:238
  447.0 25.3 %all-to-all-done.2 = f32[16,1,16384]{2,1,0:T(1,128)S(1)} async-done(((f32[16,1,16384]{2,1,0:T(1,128)}), f32[16,1,16384]{2,1,0:T(1,128)S(1)}, u32[]{:S(2)}, u32[]{:S(2)}) %all-to-all-start.2) | async-done | bytes 1048608 | tf_op jit(solution)/shard_map/all_to_all | solution.py:238
  475.9 4.8 reshape.159
  480.7 6.3 %copy.116 = f32[2048,16,1,8]{0,2,3,1:T(1,128)S(1)} copy(f32[2048,16,1,8]{1,3,2,0:T(8,128)} %bitcast.103) | data formatting | bytes 2097152 | tf_op jit(solution)/shard_map/all_to_all | solution.py:238
  (204 shorter events, 120.5 us)
Async XLA Ops:
  0.6 8.7 %copy-start.5 = (f32[3,128,128]{2,1,0:T(8,128)S(1)}, f32[3,128,128]{2,1,0:T(8,128)}, u32[]{:S(2)}) copy-start(f32[3,128,128]{2,1,0:T(8,128)} %param.14) | copy-start | bytes 589828
  3.6 19.2 %all-to-all-start = ((f32[16,128,128]{2,1,0:T(8,128)}), f32[16,128,128]{2,1,0:T(8,128)S(1)}, u32[]{:S(2)}, u32[]{:S(2)}) async-start(f32[16,128,128]{2,1,0:T(8,128)} %broadcast_in_dim.71), calls=%async_computation | async-start | bytes 2097152 | tf_op jit(solution)/shard_map/all_to_all | solution.py:24
  9.3 44.9 %copy-start = (f32[128,16,128]{2,1,0:T(8,128)S(1)}, f32[128,16,128]{2,1,0:T(8,128)}, u32[]{:S(2)}) copy-start(f32[128,16,128]{2,1,0:T(8,128)} %param.11) | copy-start | bytes 3145732
  9.4 9.0 %collective-permute-start.4 = (f32[1,128]{1,0:T(1,128)S(1)}, f32[1,128]{1,0:T(1,128)S(1)}, u32[]{:S(2)}, u32[]{:S(2)}) collective-permute-start(f32[1,128]{1,0:T(1,128)S(1)} %slice_bitcast_fusion.2), channel_id=1, source_target_pairs={{0,240},{16,0},{32,16},{48,32},{64,48},{80,64},{96,80},{112,96},{1... | collective-permute-start | bytes 1544 | tf_op jit(solution)/shard_map/ppermute | solution.py:35
  18.4 7.5 %collective-permute-start.5 = (f32[1,128]{1,0:T(1,128)S(1)}, f32[1,128]{1,0:T(1,128)S(1)}, u32[]{:S(2)}, u32[]{:S(2)}) collective-permute-start(f32[1,128]{1,0:T(1,128)S(1)} %slice.346), channel_id=1, source_target_pairs={{0,16},{16,32},{32,48},{48,64},{64,80},{80,96},{96,112},{112,128},... | collective-permute-start | bytes 1544 | tf_op jit(solution)/shard_map/ppermute | solution.py:35
  26.0 5.9 %collective-permute-start.6 = (f32[1,128]{1,0:T(1,128)S(1)}, f32[1,128]{1,0:T(1,128)S(1)}, u32[]{:S(2)}, u32[]{:S(2)}) collective-permute-start(f32[1,128]{1,0:T(1,128)S(1)} %slice.351), channel_id=1, source_target_pairs={{0,240},{16,0},{32,16},{48,32},{64,48},{80,64},{96,80},{112,96},{1... | collective-permute-start | bytes 1544 | tf_op jit(solution)/shard_map/ppermute | solution.py:35
  31.9 7.5 %collective-permute-start.7 = (f32[1,128]{1,0:T(1,128)S(1)}, f32[1,128]{1,0:T(1,128)S(1)}, u32[]{:S(2)}, u32[]{:S(2)}) collective-permute-start(f32[1,128]{1,0:T(1,128)S(1)} %slice.352), channel_id=1, source_target_pairs={{0,16},{16,32},{32,48},{48,64},{64,80},{80,96},{96,112},{112,128},... | collective-permute-start | bytes 1544 | tf_op jit(solution)/shard_map/ppermute | solution.py:35
  39.5 3.6 collective-permute-start.8
  43.2 7.2 %collective-permute-start.9 = (f32[1,128]{1,0:T(1,128)S(1)}, f32[1,128]{1,0:T(1,128)S(1)}, u32[]{:S(2)}, u32[]{:S(2)}) collective-permute-start(f32[1,128]{1,0:T(1,128)S(1)} %slice.358), channel_id=1, source_target_pairs={{0,16},{16,32},{32,48},{48,64},{64,80},{80,96},{96,112},{112,128},... | collective-permute-start | bytes 1544 | tf_op jit(solution)/shard_map/ppermute | solution.py:35
  50.5 3.6 collective-permute-start.10
  54.2 7.2 %collective-permute-start.11 = (f32[1,128]{1,0:T(1,128)S(1)}, f32[1,128]{1,0:T(1,128)S(1)}, u32[]{:S(2)}, u32[]{:S(2)}) collective-permute-start(f32[1,128]{1,0:T(1,128)S(1)} %slice.364), channel_id=1, source_target_pairs={{0,16},{16,32},{32,48},{48,64},{64,80},{80,96},{96,112},{112,128},... | collective-permute-start | bytes 1544 | tf_op jit(solution)/shard_map/ppermute | solution.py:35
  61.5 3.6 collective-permute-start.12
  65.1 13.2 %collective-permute-start.13 = (f32[1,128]{1,0:T(1,128)S(1)}, f32[1,128]{1,0:T(1,128)S(1)}, u32[]{:S(2)}, u32[]{:S(2)}) collective-permute-start(f32[1,128]{1,0:T(1,128)S(1)} %slice.370), channel_id=1, source_target_pairs={{0,16},{16,32},{32,48},{48,64},{64,80},{80,96},{96,112},{112,128},... | collective-permute-start | bytes 1544 | tf_op jit(solution)/shard_map/ppermute | solution.py:35
  70.2 40.8 %collective-permute-start = (f32[2,1,16,128]{3,2,1,0:T(8,128)S(1)}, f32[2,1,16,128]{3,2,1,0:T(8,128)S(1)}, u32[]{:S(2)}, u32[]{:S(2)}) collective-permute-start(f32[2,1,16,128]{3,2,1,0:T(8,128)S(1)} %copy.94), channel_id=1, source_target_pairs={{16,0},{32,16},{48,32},{64,48},{80,64},{96,80},{112,96},{128,112},... | collective-permute-start | bytes 49160 | tf_op jit(solution)/shard_map/ppermute | solution.py:48
  78.1 35.0 %collective-permute-start.1 = (f32[2,1,16,128]{3,2,1,0:T(8,128)S(1)}, f32[2,1,16,128]{3,2,1,0:T(8,128)S(1)}, u32[]{:S(2)}, u32[]{:S(2)}) collective-permute-start(f32[2,1,16,128]{3,2,1,0:T(8,128)S(1)} %copy.96), channel_id=1, source_target_pairs={{0,16},{16,32},{32,48},{48,64},{64,80},{80,96},{96,112},{112,128},... | collective-permute-start | bytes 49160 | tf_op jit(solution)/shard_map/ppermute | solution.py:46
  78.4 17.7 %copy-start.9 = (s32[16]{0:T(128)S(1)}, s32[16]{0:T(128)}, u32[]{:S(2)}) copy-start(s32[16]{0:T(128)} %param.16) | copy-start | bytes 196
  78.4 10.2 %collective-permute-start.14 = (f32[1,128]{1,0:T(1,128)S(1)}, f32[1,128]{1,0:T(1,128)S(1)}, u32[]{:S(2)}, u32[]{:S(2)}) collective-permute-start(f32[1,128]{1,0:T(1,128)S(1)} %slice.375), channel_id=1, source_target_pairs={{0,240},{16,0},{32,16},{48,32},{64,48},{80,64},{96,80},{112,96},{1... | collective-permute-start | bytes 1544 | tf_op jit(solution)/shard_map/ppermute | solution.py:35
  84.2 34.6 %collective-permute-start.2 = (f32[128,1,128]{0,2,1:T(8,128)S(1)}, f32[128,1,128]{0,2,1:T(8,128)S(1)}, u32[]{:S(2)}, u32[]{:S(2)}) collective-permute-start(f32[128,1,128]{0,2,1:T(8,128)S(1)} %get-tuple-element.260), channel_id=1, source_target_pairs={{1,0},{2,1},{3,2},{4,3},{5,4},{6,5},{7,6},{8,7},{9,8},{10,9},{11,1... | collective-permute-start | bytes 196616 | tf_op jit(solution)/shard_map/ppermute | solution.py:48
  86.1 32.6 %collective-permute-start.3 = (f32[128,1,128]{0,2,1:T(8,128)S(1)}, f32[128,1,128]{0,2,1:T(8,128)S(1)}, u32[]{:S(2)}, u32[]{:S(2)}) collective-permute-start(f32[128,1,128]{0,2,1:T(8,128)S(1)} %get-tuple-element.261), channel_id=1, source_target_pairs={{0,1},{1,2},{2,3},{3,4},{4,5},{5,6},{6,7},{7,8},{8,9},{9,10},{10,1... | collective-permute-start | bytes 196616 | tf_op jit(solution)/shard_map/ppermute | solution.py:46
  88.6 11.1 %copy-start.8 = (s32[16]{0:T(128)S(1)}, s32[16]{0:T(128)}, u32[]{:S(2)}) copy-start(s32[16]{0:T(128)} %param.17) | copy-start | bytes 196
  88.7 7.2 %collective-permute-start.15 = (f32[1,128]{1,0:T(1,128)S(1)}, f32[1,128]{1,0:T(1,128)S(1)}, u32[]{:S(2)}, u32[]{:S(2)}) collective-permute-start(f32[1,128]{1,0:T(1,128)S(1)} %slice.376), channel_id=1, source_target_pairs={{0,16},{16,32},{32,48},{48,64},{64,80},{80,96},{96,112},{112,128},... | collective-permute-start | bytes 1544 | tf_op jit(solution)/shard_map/ppermute | solution.py:35
  96.0 3.6 collective-permute-start.16
  99.6 7.2 %collective-permute-start.17 = (f32[1,128]{1,0:T(1,128)S(1)}, f32[1,128]{1,0:T(1,128)S(1)}, u32[]{:S(2)}, u32[]{:S(2)}) collective-permute-start(f32[1,128]{1,0:T(1,128)S(1)} %slice.382), channel_id=1, source_target_pairs={{0,16},{16,32},{32,48},{48,64},{64,80},{80,96},{96,112},{112,128},... | collective-permute-start | bytes 1544 | tf_op jit(solution)/shard_map/ppermute | solution.py:35
  107.0 3.6 collective-permute-start.18
  110.7 7.2 %collective-permute-start.19 = (f32[1,128]{1,0:T(1,128)S(1)}, f32[1,128]{1,0:T(1,128)S(1)}, u32[]{:S(2)}, u32[]{:S(2)}) collective-permute-start(f32[1,128]{1,0:T(1,128)S(1)} %slice.388), channel_id=1, source_target_pairs={{0,16},{16,32},{32,48},{48,64},{64,80},{80,96},{96,112},{112,128},... | collective-permute-start | bytes 1544 | tf_op jit(solution)/shard_map/ppermute | solution.py:35
  123.6 30.8 %all-to-all-start.1 = ((f32[128,16,16,8]{0,3,1,2:T(8,128)}), f32[128,16,16,8]{0,3,1,2:T(8,128)S(1)}, u32[]{:S(2)}, u32[]{:S(2)}) async-start(f32[128,16,16,8]{0,3,1,2:T(8,128)} %copy.109), calls=%async_computation.1 | async-start | bytes 2097152 | tf_op jit(solution)/shard_map/all_to_all | solution.py:208
  260.6 23.0 %copy-start.7 = (f32[1025]{0:T(1024)S(1)}, f32[1025]{0:T(1024)}, u32[]{:S(2)}) copy-start(f32[1025]{0:T(1024)} %param.15) | copy-start | bytes 12304
  261.8 11.2 %collective-permute-start.20 = (f32[2048,16,3]{0,2,1:T(4,128)}, f32[2048,16,3]{0,2,1:T(4,128)S(1)}, u32[]{:S(2)}, u32[]{:S(2)}) collective-permute-start(f32[2048,16,3]{0,2,1:T(4,128)} %get-tuple-element.258), channel_id=1, source_target_pairs={{0,16},{16,32},{32,48},{48,64},{64,80},{80,96},{96,112},{112,128},... | collective-permute-start | bytes 1179656 | tf_op jit(solution)/shard_map/ppermute | solution.py:46
  265.0 12.1 %collective-permute-start.21 = (f32[2048,16,3]{0,2,1:T(4,128)}, f32[2048,16,3]{0,2,1:T(4,128)S(1)}, u32[]{:S(2)}, u32[]{:S(2)}) collective-permute-start(f32[2048,16,3]{0,2,1:T(4,128)} %get-tuple-element.259), channel_id=1, source_target_pairs={{16,0},{32,16},{48,32},{64,48},{80,64},{96,80},{112,96},{128,112},... | collective-permute-start | bytes 1179656 | tf_op jit(solution)/shard_map/ppermute | solution.py:48
  278.1 13.5 %collective-permute-start.22 = (f32[2048,3,14]{0,2,1:T(8,128)}, f32[2048,3,14]{0,2,1:T(8,128)S(1)}, u32[]{:S(2)}, u32[]{:S(2)}) collective-permute-start(f32[2048,3,14]{0,2,1:T(8,128)} %get-tuple-element.254), channel_id=1, source_target_pairs={{0,1},{1,2},{2,3},{3,4},{4,5},{5,6},{6,7},{7,8},{8,9},{9,10},{10,1... | collective-permute-start | bytes 1032200 | tf_op jit(solution)/shard_map/ppermute | solution.py:46
  280.0 11.6 %collective-permute-start.23 = (f32[2048,3,14]{0,2,1:T(8,128)}, f32[2048,3,14]{0,2,1:T(8,128)}, u32[]{:S(2)}, u32[]{:S(2)}) collective-permute-start(f32[2048,3,14]{0,2,1:T(8,128)} %get-tuple-element.255), channel_id=1, source_target_pairs={{1,0},{2,1},{3,2},{4,3},{5,4},{6,5},{7,6},{8,7},{9,8},{10,9},{11,1... | collective-permute-start | bytes 1032200 | tf_op jit(solution)/shard_map/ppermute | solution.py:48
  438.0 34.2 %all-to-all-start.2 = ((f32[16,1,16384]{2,1,0:T(1,128)}), f32[16,1,16384]{2,1,0:T(1,128)S(1)}, u32[]{:S(2)}, u32[]{:S(2)}) async-start(f32[16,1,16384]{2,1,0:T(1,128)} %reshape.158), calls=%async_computation.2 | async-start | bytes 2097152 | tf_op jit(solution)/shard_map/all_to_all | solution.py:238
  (5 other events, 40.9 us)
where the time goes:
time: 499 us; the launch traced here: 489 us
  matrix products  191 us (38%)
  waiting for transfers between devices  126 us (25%)
  local copies, waits for them, and re-layouts  78.2 us (16%)
  starting transfers between devices  62 us (12%)
  other arithmetic  24.2 us (5%)
  loops' own time  5.83 us (1%)
    dot_general x4, matrix products, inverse_one_block(): lax.dot_general(basis, weighted, (((0,), (0,)), ((), ())), precision=lax....  103 us
    dot_general x4, matrix products, forward_one_block(): jnp.dot(basis, columns, precision=lax.Precision.HIGHEST, preferred_elemen...  87.2 us
    ppermute x16, waiting for transfers between devices, passed_along(): return lax.ppermute(value, axis, pairs)  51.7 us
    all_to_all x1, waiting for transfers between devices, shards(): lax.all_to_all(forcing.reshape(cells_theta, cells_radius, sectors, axial_...  26.6 us
    all_to_all x1, waiting for transfers between devices, shards(): lax.all_to_all(pressure_lines, 'sector', split_axis=0, concat_axis=2, til...  25.3 us
    ppermute x16, starting transfers between devices, passed_along(): return lax.ppermute(value, axis, pairs)  25.1 us
    dynamic_update_slice x16, local copies, waits for them, and re-layouts, forward_transform(): result = lax.map(forward_one_block, jnp.arange(count, dtype=jnp.int32))  20.9 us
    unnamed x29, local copies, waits for them, and re-layouts  19.7 us
  transfers between devices with their start and end apart: 27, of which 20 were waited for; matrix products, arithmetic and copies ran while one was open for 4% of the time, Pallas kernels for 0%

commit v1 on v0

v1 whole, which is shorter than its diff:
```python
import math

import jax
import jax.numpy as jnp
import numpy as np
from jax import lax
from jax.experimental import pallas as pl
from jax.experimental.pallas import tpu as pltpu
from jax.sharding import PartitionSpec as P

MOUTH = 8
SWEEPS = 4
SUBSTEPS = 8
REACH = SWEEPS - 1
NT, NR, NZ = 2048, 256, 128
SECTORS, RADIALS = 16, 16
T = NT // SECTORS
R = NR // RADIALS
Q = NZ // SECTORS
TILES = 8
WIDE = 2 * T
CHUNKS = ((0, 4), (12, 4), (4, 4), (8, 4))

F32, BF16 = jnp.float32, jnp.bfloat16


def halves(table):
    high = table.astype(BF16)
    low = (table - high.astype(np.float64)).astype(BF16)
    return np.stack([high, low])


def mode_tables():
    j = np.arange(T)
    a = np.arange(T)
    tiles = np.zeros((TILES, WIDE, WIDE))
    mode = np.zeros((TILES, WIDE), np.int64)
    for k in range(1, TILES):
        order = SECTORS * a + k
        phase = 2 * np.pi * ((j[:, None] * order[None, :]) % NT) / NT
        tiles[k, :T, :T], tiles[k, :T, T:] = np.cos(phase), np.sin(phase)
        tiles[k, T:, :T], tiles[k, T:, T:] = -np.sin(phase), np.cos(phase)
        mode[k] = np.concatenate([order, order])
    low_cos, low_sin = SECTORS * np.arange(T // 2 + 1), SECTORS * np.arange(1, T // 2)
    mid = SECTORS * np.arange(T // 2) + SECTORS // 2

    def phase_of(order):
        return 2 * np.pi * ((j[:, None] * order[None, :]) % NT) / NT

    tiles[0, :T, :T] = np.concatenate([np.cos(phase_of(low_cos)), np.sin(phase_of(low_sin))], 1)
    tiles[0, T:, T:] = np.concatenate([np.cos(phase_of(mid)), np.sin(phase_of(mid))], 1)
    mode[0] = np.concatenate([low_cos, low_sin, mid, mid])
    mode = np.minimum(mode, NT - mode)
    weight = np.where((mode == 0) | (mode == NT // 2), 1.0, 2.0) / NT
    return tiles, mode.reshape(-1), weight.reshape(-1)


def axial_tables():
    n = np.arange(1, NZ + 1)
    sines = math.sqrt(2.0 / (NZ + 1)) * np.sin(np.pi * ((n[:, None] * n[None, :]) % (2 * (NZ + 1))) / (NZ + 1))
    return sines, 2.0 * np.cos(np.pi * n / (NZ + 1))


C1, C2, C3 = (math.cos(math.pi * n / 8) for n in (1, 2, 3))


def cosine_stage(e):
    f = [e[n] + e[8 - n] for n in range(4)] + [e[4]]
    g = [e[n] - e[8 - n] for n in range(4)]
    outer, inner = f[0] + f[4], f[1] + f[3]
    differ, h = f[0] - f[4], C2 * (f[1] - f[3])
    both = outer + f[2]
    w = C2 * g[2]
    up, down = g[0] + w, g[0] - w
    b, c = C1 * g[1] + C3 * g[3], C3 * g[1] - C1 * g[3]
    return [both + inner, up + b, differ + h, down + c, outer - f[2], down - c, differ - h, up - b, both - inner]


def sine_stage(o):
    u = [None] + [o[n] + o[8 - n] for n in (1, 2, 3)] + [o[4]]
    v = [None] + [o[n] - o[8 - n] for n in (1, 2, 3)]
    h = C2 * (v[1] + v[3])
    w = C2 * u[2]
    up, down = w + u[4], w - u[4]
    b, c = C3 * u[1] + C1 * u[3], C1 * u[1] - C3 * u[3]
    return [None, b + up, h + v[2], c + down, v[1] - v[3], c - down, h - v[2], b - up]


def split(x):
    high = x.astype(BF16)
    return high, (x - high.astype(F32)).astype(BF16)


def product(left, right, dims=((1,), (0,))):
    def one(a, b):
        return lax.dot_general(a, b, (dims, ((), ())), preferred_element_type=F32)

    return one(left[0], right[0]) + (one(left[0], right[1]) + one(left[1], right[0]))


def rows_of(r):
    return pl.ds(r, T, stride=R)


def kernel(
    azimuth, radius, dens_hbm, swirl_hbm, heat_hbm, ac_hbm, inverse, lam, sines, fwd_hbm, bwd_hbm,
    dn_hbm, press_hbm, acn_hbm,
    dext, sext, heat, acx, hext, rsend, rhalo, tmask, srcbuf, agbuf, acn, psend, precv, phat,
    send1, recv1, send2, recv2, modes, yhi, ylo, xhi, xlo, zbuf, dn, press, fwd, bwd,
    load_sem, store_sem, halo_s, halo_r, rs_s, rs_r, ag_s, ag_r, pq_s, pq_r, f_s, f_r, b_s, b_r,
):
    s, rho = lax.axis_index("sector"), lax.axis_index("radial")
    after, before = lax.rem(s + 1, SECTORS), lax.rem(s + SECTORS - 1, SECTORS)
    inner, outer = lax.rem(rho + RADIALS - 1, RADIALS), lax.rem(rho + 1, RADIALS)

    def remote(src, dst, send, recv, **where):
        return pltpu.make_async_remote_copy(
            src_ref=src, dst_ref=dst, send_sem=send, recv_sem=recv, device_id=where, device_id_type=pl.DeviceIdType.MESH
        )

    def others(body):
        def step(i, carry):
            body(i)
            return carry

        lax.fori_loop(1, SECTORS, step, 0)

    loads = [
        pltpu.make_async_copy(dens_hbm, dext.at[pl.ds(R, T * R)], load_sem.at[0]),
        pltpu.make_async_copy(heat_hbm, heat, load_sem.at[1]),
        pltpu.make_async_copy(swirl_hbm, sext.at[pl.ds(R, T * R)], load_sem.at[2]),
        pltpu.make_async_copy(ac_hbm, acx.at[:, pl.ds(8, T)], load_sem.at[3]),
        pltpu.make_async_copy(fwd_hbm, fwd, load_sem.at[4]),
        pltpu.make_async_copy(bwd_hbm, bwd, load_sem.at[5]),
    ]
    for load in loads:
        load.start()

    barrier = pltpu.get_barrier_semaphore()

    def greet(i):
        pl.semaphore_signal(barrier, inc=1, device_id={"sector": lax.rem(s + i, SECTORS)}, device_id_type=pl.DeviceIdType.MESH)
        pl.semaphore_signal(barrier, inc=1, device_id={"radial": lax.rem(rho + i, RADIALS)}, device_id_type=pl.DeviceIdType.MESH)

    others(greet)
    pl.semaphore_wait(barrier, 2 * (SECTORS - 1))

    head, tail = pl.ds(0, R), pl.ds(T * R + R, R)
    azimuth_halos = [
        remote(dens_hbm.at[pl.ds(0, R)], dext.at[tail], halo_s.at[0], halo_r.at[0], sector=before),
        remote(dens_hbm.at[pl.ds(T * R - R, R)], dext.at[head], halo_s.at[1], halo_r.at[1], sector=after),
        remote(swirl_hbm.at[pl.ds(0, R)], sext.at[tail], halo_s.at[2], halo_r.at[2], sector=before),
        remote(swirl_hbm.at[pl.ds(T * R - R, R)], sext.at[head], halo_s.at[3], halo_r.at[3], sector=after),
    ]
    wave_halos = [
        remote(ac_hbm.at[:, pl.ds(0, 8)], acx.at[:, pl.ds(T + 8, 8)], halo_s.at[4], halo_r.at[4], sector=before),
        remote(ac_hbm.at[:, pl.ds(T - 8, 8)], acx.at[:, pl.ds(0, 8)], halo_s.at[5], halo_r.at[5], sector=after),
    ]
    for copy in azimuth_halos:
        copy.start()

    loads[0].wait()
    to_inner = remote(rsend.at[0], rhalo.at[1], halo_s.at[6], halo_r.at[6], radial=inner)
    to_outer = remote(rsend.at[1], rhalo.at[0], halo_s.at[7], halo_r.at[7], radial=outer)
    rsend[0] = dext[pl.ds(R, T, stride=R), :]
    rsend[1] = dext[pl.ds(2 * R - 1, T, stride=R), :]

    @pl.when(rho > 0)
    def _():
        to_inner.start()

    @pl.when(rho < RADIALS - 1)
    def _():
        to_outer.start()

    for copy in wave_halos:
        copy.start()

    loads[1].wait()

    def heat_row(r, total):
        d = dext[pl.ds(R + r, T, stride=R), :]
        return total + heat[rows_of(r), :] * d * d

    hext[8 : 8 + T, :] = lax.fori_loop(0, R, heat_row, jnp.zeros((T, NZ), F32)) * (1.0 / NR)
    heat_halos = [
        remote(hext.at[pl.ds(8, 8)], hext.at[pl.ds(T + 8, 8)], halo_s.at[8], halo_r.at[8], sector=before),
        remote(hext.at[pl.ds(T, 8)], hext.at[pl.ds(0, 8)], halo_s.at[9], halo_r.at[9], sector=after),
    ]
    for copy in heat_halos:
        copy.start()

    theta = lax.broadcasted_iota(jnp.int32, (T, NZ), 0)
    first = azimuth[s]
    tmask[...] = jnp.where((theta >= first) & (theta < first + MOUTH), 1.0, 0.0).astype(F32)
    lane = lax.broadcasted_iota(jnp.int32, (T, NZ), 1)
    loads[2].wait()
    for copy in azimuth_halos:
        copy.wait_recv()

    @pl.when(rho > 0)
    def _():
        to_outer.wait_recv()

    @pl.when(rho == 0)
    def _():
        rhalo[0] = jnp.zeros((T, NZ), F32)

    @pl.when(rho < RADIALS - 1)
    def _():
        to_inner.wait_recv()

    @pl.when(rho == RADIALS - 1)
    def _():
        rhalo[1] = jnp.zeros((T, NZ), F32)

    sine_pair = (sines[0], sines[1])

    def flow_row(r, below, above):
        d = dext[pl.ds(R + r, T, stride=R), :]
        up = dext[pl.ds(2 * R + r, T, stride=R), :]
        down = dext[pl.ds(r, T, stride=R), :]
        axial = jnp.where(lane < NZ - 1, pltpu.roll(d, NZ - 1, 1), 0.0) + jnp.where(lane > 0, pltpu.roll(d, 1, 1), 0.0)
        laplace = (up + down) + (below + above) + axial - 6.0 * d
        flux = sext[pl.ds(2 * R + r, T, stride=R), :] * up - sext[pl.ds(r, T, stride=R), :] * down
        where = rho * R + r - radius[s]
        mouth = jnp.where((where >= 0) & (where < MOUTH), 2.5, 0.0).astype(F32)
        change = 0.05 * laplace - 0.5 * flux + (mouth * tmask[...]) * (1.0 - d)
        dn[rows_of(r), :] = d + 0.2 * change
        lines = product(sine_pair, split(change), ((1,), (1,)))
        send1[:, r] = lines.reshape(SECTORS, Q, T)

    def flow_inside(r, carry):
        flow_row(r, dext[pl.ds(R + r - 1, T, stride=R), :], dext[pl.ds(R + r + 1, T, stride=R), :])
        return carry

    def flow_chunk(c):
        start, count = CHUNKS[c]
        lo, hi = max(start, 1), min(start + count, R - 1)
        if start == 0:
            flow_row(0, rhalo[0], dext[pl.ds(R + 1, T, stride=R), :])
        lax.fori_loop(lo, hi, flow_inside, 0)
        if start + count == R:
            flow_row(R - 1, dext[pl.ds(2 * R - 2, T, stride=R), :], rhalo[1])
        part = pl.ds(start, count)
        others(
            lambda i: remote(
                send1.at[lax.rem(s + i, SECTORS), part], recv1.at[s, part], f_s.at[c, lax.rem(s + i, SECTORS)], f_r.at[c, s],
                sector=lax.rem(s + i, SECTORS),
            ).start()
        )
        recv1[s, part] = send1[s, part]

    def tile_rows(peer):
        return pl.ds(pl.multiple_of(8 * peer, 8), 24)

    def share_heat(i):
        peer = lax.rem(rho + i, RADIALS)
        return remote(hext.at[tile_rows(peer)], srcbuf.at[rho], rs_s.at[peer], rs_r.at[rho], radial=peer)

    def share_wave(i):
        peer = lax.rem(rho + i, RADIALS)
        return remote(agbuf.at[rho], agbuf.at[rho], ag_s.at[peer], ag_r.at[rho], radial=peer)

    def share_press(i):
        peer = lax.rem(s + i, SECTORS)
        return remote(psend.at[peer], precv.at[s], pq_s.at[peer], pq_r.at[s], sector=peer)

    flow_chunk(0)

    for copy in heat_halos + wave_halos:
        copy.wait_recv()
    loads[3].wait()
    others(lambda i: share_heat(i).start())
    srcbuf[rho] = hext[tile_rows(rho), :]

    flow_chunk(1)

    def arrived(buffer, send, recv, index, **where):
        remote(buffer, buffer, send, recv.at[index], **where).wait_recv()

    def heat_in(i):
        peer = lax.rem(rho + i, RADIALS)
        arrived(srcbuf.at[peer], rs_s.at[peer], rs_r, peer, radial=peer)

    others(heat_in)
    source = srcbuf[0]
    for i in range(1, RADIALS):
        source = source + srcbuf[i]
    source = 0.5 * source
    wave = [acx[n, tile_rows(rho), :] for n in range(3)]
    lane24 = lax.broadcasted_iota(jnp.int32, (24, NZ), 1)
    p, u, w = wave
    for _ in range(SUBSTEPS):
        u = u - 0.5 * (pltpu.roll(p, 23, 0) - p)
        w = w - 0.5 * (jnp.where(lane24 < NZ - 1, pltpu.roll(p, NZ - 1, 1), 0.0) - p)
        along, axial = u - pltpu.roll(u, 1, 0), w - jnp.where(lane24 > 0, pltpu.roll(w, 1, 1), 0.0)
        p = p - 0.5 * (along + axial) + source
    for n, field in enumerate((p, u, w)):
        agbuf[rho, n] = field[8:16]
    others(lambda i: share_wave(i).start())

    flow_chunk(2)

    def wave_in(i):
        peer = lax.rem(rho + i, RADIALS)
        arrived(agbuf.at[peer], ag_s.at[peer], ag_r, peer, radial=peer)

    others(wave_in)
    for n in range(3):
        acn[n] = agbuf[:, n].reshape(T, NZ)
    stores = [
        pltpu.make_async_copy(acn, acn_hbm, store_sem.at[0]),
        pltpu.make_async_copy(dn, dn_hbm, store_sem.at[1]),
        pltpu.make_async_copy(press, press_hbm, store_sem.at[2]),
    ]
    stores[0].start()
    psend[...] = product(sine_pair, split(0.5 * acn[0]), ((1,), (1,))).reshape(SECTORS, Q, T)
    others(lambda i: share_press(i).start())
    precv[s] = psend[s]

    flow_chunk(3)
    stores[1].start()
    loads[4].wait()

    def first_stage(x):
        e = [x[0]] + [x[n] + x[SECTORS - n] for n in range(1, 8)] + [x[8]]
        o = [None] + [x[n] - x[SECTORS - n] for n in range(1, 8)]
        return cosine_stage(e), sine_stage(o)

    def keep(row, values):
        cosines, sines_ = values
        at = pl.ds(row, 2 * Q)
        for k in range(TILES):
            pair = (cosines[0], cosines[8]) if k == 0 else (cosines[k], sines_[k])
            for half, value in enumerate(pair):
                high, low = split(value)
                yhi[k, at, T * half : T * half + T] = high
                ylo[k, at, T * half : T * half + T] = low

    def second_stage(rows, table, k):
        return product((yhi[k, rows, :], ylo[k, rows, :]), (table[0, k], table[1, k]))

    def mode_lanes(k):
        return pl.ds(pl.multiple_of(k * WIDE, WIDE), WIDE)

    def forward_chunk(c):
        start, count = CHUNKS[c]
        part = pl.ds(start, count)

        def lines_in(i):
            peer = lax.rem(s + i, SECTORS)
            arrived(recv1.at[peer, part], f_s.at[c, peer], f_r, (c, peer), sector=peer)

        others(lines_in)

        def pair(i, carry):
            r = start + 2 * i
            x = [recv1[n, pl.ds(r, 2)].reshape(2 * Q, T) for n in range(SECTORS)]
            keep(pl.multiple_of(r * Q, 2 * Q), first_stage(x))
            return carry

        lax.fori_loop(0, count // 2, pair, 0)

        def tile(k, carry):
            out = second_stage(pl.ds(start * Q, count * Q), fwd, k)
            modes[pl.ds(REACH + start, count), :, mode_lanes(k)] = out.reshape(count, Q, WIDE)
            return carry

        lax.fori_loop(0, TILES, tile, 0)

    modes_inner = remote(modes.at[pl.ds(REACH, REACH)], modes.at[pl.ds(REACH + R, REACH)], halo_s.at[10], halo_r.at[10], radial=inner)
    modes_outer = remote(modes.at[pl.ds(R, REACH)], modes.at[pl.ds(0, REACH)], halo_s.at[11], halo_r.at[11], radial=outer)

    forward_chunk(0)

    @pl.when(rho > 0)
    def _():
        modes_inner.start()

    forward_chunk(1)

    @pl.when(rho < RADIALS - 1)
    def _():
        modes_outer.start()

    forward_chunk(2)
    forward_chunk(3)

    def press_in(i):
        peer = lax.rem(s + i, SECTORS)
        arrived(precv.at[peer], pq_s.at[peer], pq_r, peer, sector=peer)

    others(press_in)
    both = [jnp.concatenate([precv[n], precv[n]], 0) for n in range(SECTORS)]
    keep(T, first_stage(both))

    def press_tile(k, carry):
        phat[:, mode_lanes(k)] = second_stage(pl.ds(T, 2 * Q), fwd, k)[:Q]
        return carry

    lax.fori_loop(0, TILES, press_tile, 0)

    @pl.when(rho > 0)
    def _():
        modes_outer.wait_recv()

    @pl.when(rho == 0)
    def _():
        modes[0:REACH] = jnp.zeros((REACH, Q, NT), F32)

    @pl.when(rho < RADIALS - 1)
    def _():
        modes_inner.wait_recv()

    @pl.when(rho == RADIALS - 1)
    def _():
        modes[REACH + R : R + 2 * REACH] = jnp.zeros((REACH, Q, NT), F32)

    axial_sum = lam[pl.ds(pl.multiple_of(s * Q, Q), Q), :]
    keep_low = jnp.where(rho > 0, 1.0, 0.0).astype(F32)
    keep_high = jnp.where(rho < RADIALS - 1, 1.0, 0.0).astype(F32)

    def solve(block, carry):
        at = pl.ds(pl.multiple_of(block * T, T), T)
        inv = jnp.broadcast_to(inverse[0:1, at], (Q, T))
        last = jnp.broadcast_to(inverse[1:2, at], (Q, T))
        total = R + 2 * REACH
        scale = [inv * keep_low] * REACH + [inv] * R + [inv * keep_high] * REACH
        extra = phat[:, at]
        ends = [extra * keep_low] * REACH + [extra] * R + [extra * keep_high] * REACH
        c = [modes[n, :, at] + ends[n] for n in range(total)]
        x = [c[n] * scale[n] for n in range(total)]
        for sweep in range(1, SWEEPS):
            x = [
                None
                if n < sweep or n >= total - sweep
                else ((c[n] + axial_sum * x[n]) + (x[n - 1] + x[n + 1])) * (last if sweep == SWEEPS - 1 else scale[n])
                for n in range(total)
            ]
        for n in range(0, R, 2):
            high, low = split(jnp.concatenate([x[REACH + n], x[REACH + n + 1]], 0))
            xhi[n * Q : n * Q + 2 * Q, at] = high
            xlo[n * Q : n * Q + 2 * Q, at] = low
        return carry

    lax.fori_loop(0, NT // T, solve, 0)
    loads[5].wait()

    def backward_chunk(c):
        start, count = CHUNKS[c]
        rows, part = pl.ds(start * Q, count * Q), pl.ds(start, count)

        def tile(k, carry):
            at = mode_lanes(k)
            zbuf[k, rows, :] = product((xhi[rows, at], xlo[rows, at]), (bwd[0, k], bwd[1, k]))
            return carry

        lax.fori_loop(0, TILES, tile, 0)

        def row(i, carry):
            r = start + i
            at = pl.ds(pl.multiple_of(r * Q, Q), Q)
            z = [(zbuf[k, at, 0:T], zbuf[k, at, T:WIDE]) for k in range(TILES)]
            even = cosine_stage([z[0][0]] + [z[k][0] for k in range(1, TILES)] + [z[0][1]])
            odd = sine_stage([None] + [z[k][1] for k in range(1, TILES)])
            send2[0, r], send2[8, r] = even[0], even[8]
            for n in range(1, 8):
                send2[n, r] = even[n] + odd[n]
                send2[SECTORS - n, r] = even[n] - odd[n]
            return carry

        lax.fori_loop(0, count, row, 0)
        others(
            lambda i: remote(
                send2.at[lax.rem(s + i, SECTORS), part], recv2.at[s, part], b_s.at[c, lax.rem(s + i, SECTORS)], b_r.at[c, s],
                sector=lax.rem(s + i, SECTORS),
            ).start()
        )
        recv2[s, part] = send2[s, part]

    for c in range(len(CHUNKS)):
        backward_chunk(c)

    for c, (start, count) in enumerate(CHUNKS):
        part = pl.ds(start, count)

        def lines_back(i, c=c, part=part):
            peer = lax.rem(s + i, SECTORS)
            arrived(recv2.at[peer, part], b_s.at[c, peer], b_r, (c, peer), sector=peer)

        others(lines_back)

        def finish(r, carry):
            lines = recv2[:, r].reshape(NZ, T).T
            press[rows_of(r), :] = product(split(lines), sine_pair)
            return carry

        lax.fori_loop(start, start + count, finish, 0)
    stores[2].start()

    for copy in azimuth_halos + wave_halos + heat_halos:
        copy.wait_send()

    @pl.when(rho > 0)
    def _():
        to_inner.wait_send()
        modes_inner.wait_send()

    @pl.when(rho < RADIALS - 1)
    def _():
        to_outer.wait_send()
        modes_outer.wait_send()

    def sent(i):
        share_heat(i).wait_send()
        share_wave(i).wait_send()
        share_press(i).wait_send()
        peer = lax.rem(s + i, SECTORS)
        for c, (start, count) in enumerate(CHUNKS):
            part = pl.ds(start, count)
            remote(send1.at[peer, part], recv1.at[s, part], f_s.at[c, peer], f_r.at[c, s], sector=peer).wait_send()
            remote(send2.at[peer, part], recv2.at[s, part], b_s.at[c, peer], b_r.at[c, s], sector=peer).wait_send()

    others(sent)
    for store in stores:
        store.wait()


def shards(density, swirl, heat_rate, acoustic, mode_impedance, mouth_azimuth, mouth_radius):
    tiles, mode, weight = mode_tables()
    sines, axial_sum = axial_tables()
    half = NT // 2
    whole = jnp.concatenate([mode_impedance, mode_impedance[1:half][::-1]]).reshape(T, SECTORS).T
    by_lane = jnp.concatenate(
        [whole[0, : T // 2 + 1], whole[0, 1 : T // 2], whole[8, : T // 2], whole[8, : T // 2]]
        + [whole[k] for k in range(1, TILES) for _ in range(2)]
    )
    diagonal = jnp.asarray((4.0 + 2.0 - 2.0 * np.cos(2 * np.pi * mode / NT)).astype(np.float32)) + by_lane
    inverse = 1.0 / diagonal
    inverse = jnp.stack([inverse, inverse * jnp.asarray(weight.astype(np.float32))])
    lam = jnp.asarray(np.repeat(axial_sum[:, None], T, 1).astype(np.float32))
    flat = lambda x: x.reshape(T * R, NZ)
    vmem, smem, anywhere = (pl.BlockSpec(memory_space=m) for m in (pltpu.VMEM, pltpu.SMEM, pl.ANY))
    dma = pltpu.SemaphoreType.DMA
    dn, press, acn = pl.pallas_call(
        kernel,
        out_shape=(
            jax.ShapeDtypeStruct((T * R, NZ), F32),
            jax.ShapeDtypeStruct((T * R, NZ), F32),
            jax.ShapeDtypeStruct((3, T, NZ), F32),
        ),
        in_specs=[smem, smem] + [anywhere] * 4 + [vmem] * 3 + [anywhere] * 2,
        out_specs=(anywhere, anywhere, anywhere),
        scratch_shapes=[
            pltpu.VMEM(((T + 2) * R, NZ), F32),
            pltpu.VMEM(((T + 2) * R, NZ), F32),
            pltpu.VMEM((T * R, NZ), F32),
            pltpu.VMEM((3, T + 16, NZ), F32),
            pltpu.VMEM((T + 16, NZ), F32),
            pltpu.VMEM((2, T, NZ), F32),
            pltpu.VMEM((2, T, NZ), F32),
            pltpu.VMEM((T, NZ), F32),
            pltpu.VMEM((RADIALS, 24, NZ), F32),
            pltpu.VMEM((RADIALS, 3, 8, NZ), F32),
            pltpu.VMEM((3, T, NZ), F32),
            pltpu.VMEM((SECTORS, Q, T), F32),
            pltpu.VMEM((SECTORS, Q, T), F32),
            pltpu.VMEM((Q, NT), F32),
            pltpu.VMEM((SECTORS, R, Q, T), F32),
            pltpu.VMEM((SECTORS, R, Q, T), F32),
            pltpu.VMEM((SECTORS, R, Q, T), F32),
            pltpu.VMEM((SECTORS, R, Q, T), F32),
            pltpu.VMEM((R + 2 * REACH, Q, NT), F32),
            pltpu.VMEM((TILES, R * Q + 2 * Q, WIDE), BF16),
            pltpu.VMEM((TILES, R * Q + 2 * Q, WIDE), BF16),
            pltpu.VMEM((R * Q, NT), BF16),
            pltpu.VMEM((R * Q, NT), BF16),
            pltpu.VMEM((TILES, R * Q, WIDE), F32),
            pltpu.VMEM((T * R, NZ), F32),
            pltpu.VMEM((T * R, NZ), F32),
            pltpu.VMEM((2, TILES, WIDE, WIDE), BF16),
            pltpu.VMEM((2, TILES, WIDE, WIDE), BF16),
            dma((6,)),
            dma((3,)),
            dma((12,)),
            dma((12,)),
            dma((RADIALS,)),
            dma((RADIALS,)),
            dma((RADIALS,)),
            dma((RADIALS,)),
            dma((SECTORS,)),
            dma((SECTORS,)),
            dma((len(CHUNKS), SECTORS)),
            dma((len(CHUNKS), SECTORS)),
            dma((len(CHUNKS), SECTORS)),
            dma((len(CHUNKS), SECTORS)),
        ],
        compiler_params=pltpu.CompilerParams(collective_id=0, has_side_effects=True, vmem_limit_bytes=48 * 2**20),
    )(
        mouth_azimuth, mouth_radius, flat(density), flat(swirl), flat(heat_rate), acoustic, inverse, lam,
        jnp.asarray(halves(sines)), jnp.asarray(halves(tiles)), jnp.asarray(halves(tiles.transpose(0, 2, 1))),
    )
    return dn.reshape(T, R, NZ), press.reshape(T, R, NZ), acn


def solution(mesh):
    cells, columns = P("sector", "radial", None), P(None, "sector", None)
    return jax.shard_map(
        shards,
        mesh=mesh,
        in_specs=(cells, cells, cells, columns, P(), P(), P()),
        out_specs=(cells, cells, columns),
        check_vma=False,
    )
```

time: 499 us -> 96.8 us (0.19)
  the two profiles are of different devices: /device:TPU:10 before, /device:TPU:8 now
where the time goes in v1:
time: 96.8 us; the launch traced here: 95.3 us
  Pallas kernels  81.1 us (84%)
  local copies, waits for them, and re-layouts  12 us (12%)
  other arithmetic  1.51 us (2%)
    pallas_call x1, Pallas kernels, shards(): pl.pallas_call(kernel, out_shape=(jax.ShapeDtypeStruct((T * R, NZ), F32),...  81.1 us
    unnamed x21, local copies, waits for them, and re-layouts  10.4 us

profile of v1, /device:TPU:8, one launch (start us, length us, event | category | flops | bytes accessed | tf_op | source)
XLA Modules:
  0.0 95.3 jit_solution(18265011236997425679)
XLA Ops:
  0.6 0.8 slice.41
  1.4 0.1 reverse
  1.5 0.1 slice.72
  1.5 0.8 pad_maximum_fusion.1
  2.3 0.1 reshape.27
  2.4 0.2 slice_reduce_fusion.8
  2.6 0.1 slice_reduce_fusion.9
  2.7 0.1 slice_reduce_fusion.7
  2.8 0.4 slice_reduce_fusion
  3.2 0.1 concatenate.7
  3.3 0.7 add_divide_fusion
  4.0 0.0 copy-start
  4.0 1.2 %copy-done = f32[128,16,128]{2,1,0:T(8,128)S(1)} copy-done((f32[128,16,128]{2,1,0:T(8,128)S(1)}, f32[128,16,128]{2,1,0:T(8,128)}, u32[]{:S(2)}) %copy-start) | copy-done | bytes 1048600
  5.2 0.0 copy-start.1
  5.3 1.2 %copy-done.1 = f32[128,16,128]{2,1,0:T(8,128)S(1)} copy-done((f32[128,16,128]{2,1,0:T(8,128)S(1)}, f32[128,16,128]{2,1,0:T(8,128)}, u32[]{:S(2)}) %copy-start.1) | copy-done | bytes 1048600
  6.5 0.0 copy-start.2
  6.5 1.2 %copy-done.2 = f32[128,16,128]{2,1,0:T(8,128)S(1)} copy-done((f32[128,16,128]{2,1,0:T(8,128)S(1)}, f32[128,16,128]{2,1,0:T(8,128)}, u32[]{:S(2)}) %copy-start.2) | copy-done | bytes 1048600
  7.7 0.0 copy-start.3
  7.7 0.9 copy-done.3
  8.6 0.0 copy-start.4
  8.6 0.8 copy-done.4
  9.5 0.0 copy-start.5
  9.5 0.8 copy-done.5
  10.3 0.0 copy-start.6
  10.3 0.7 copy-done.6
  11.0 0.0 copy-start.7
  11.0 0.7 copy-done.7
  11.6 81.1 %shard_map.148 = (f32[2048,128]{1,0:T(8,128)S(1)}, f32[2048,128]{1,0:T(8,128)S(1)}, f32[3,128,128]{2,1,0:T(8,128)S(1)}) custom-call(s32[16]{0:T(128)S(1)} %copy-done.6, s32[16]{0:T(128)S(1)} %copy-done.7, f32[2048,128]{1,0:T(8,128)S(1)} %bitcast.11, f32[2048,128]{1,0:T(8,128)S(1)} %bitcast.12, f32[2048,128]{1,0:T(8,128)S(1)} %bitcast.13, ...), custom_call_target="tpu_custom_call" | custom-call | tf_op jit(solution)/shard_map/pallas_call | solution.py:546
  92.7 1.0 %copy.19 = f32[128,16,128]{2,1,0:T(8,128)} copy(f32[128,16,128]{2,1,0:T(8,128)S(1)} %bitcast.10) | data formatting | bytes 2097152
  93.7 1.0 %copy.20 = f32[128,16,128]{2,1,0:T(8,128)} copy(f32[128,16,128]{2,1,0:T(8,128)S(1)} %bitcast.9) | data formatting | bytes 2097152
  94.6 0.7 copy.21
  (1 shorter events, 0.0 us)
Async XLA Ops:
  4.0 1.2 %copy-start = (f32[128,16,128]{2,1,0:T(8,128)S(1)}, f32[128,16,128]{2,1,0:T(8,128)}, u32[]{:S(2)}) copy-start(f32[128,16,128]{2,1,0:T(8,128)} %param.13) | copy-start | bytes 3145732
  5.2 1.2 %copy-start.1 = (f32[128,16,128]{2,1,0:T(8,128)S(1)}, f32[128,16,128]{2,1,0:T(8,128)}, u32[]{:S(2)}) copy-start(f32[128,16,128]{2,1,0:T(8,128)} %param.14) | copy-start | bytes 3145732
  6.5 1.2 %copy-start.2 = (f32[128,16,128]{2,1,0:T(8,128)S(1)}, f32[128,16,128]{2,1,0:T(8,128)}, u32[]{:S(2)}) copy-start(f32[128,16,128]{2,1,0:T(8,128)} %param.15) | copy-start | bytes 3145732
  7.7 0.9 copy-start.3
  8.6 0.8 copy-start.4
  9.5 0.8 copy-start.5
  10.3 0.7 copy-start.6
  11.0 0.7 copy-start.7

commit v2 on v1

v2 whole, which is shorter than its diff:
```python
import math

import jax
import jax.numpy as jnp
import numpy as np
from jax import lax
from jax.experimental import pallas as pl
from jax.experimental.pallas import tpu as pltpu
from jax.sharding import PartitionSpec as P

MOUTH = 8
SWEEPS = 4
SUBSTEPS = 8
REACH = SWEEPS - 1
NT, NR, NZ = 2048, 256, 128
SECTORS, RADIALS = 16, 16
T = NT // SECTORS
R = NR // RADIALS
Q = NZ // SECTORS
TILES = 8
WIDE = 2 * T
BURNERS = 16
EDGE = 4
SENDS = ((0, 4), (4, 4), (8, 4), (12, 4))
RETURNS = ((0, 4), (4, 6), (10, 4), (14, 2))
VMEM_LIMIT = 48 * 2**20

F32, BF16 = jnp.float32, jnp.bfloat16


def halves(table):
    high = table.astype(BF16)
    low = (table - high.astype(np.float64)).astype(BF16)
    return np.stack([high, low])


def mode_tables():
    j = np.arange(T)
    a = np.arange(T)
    tiles = np.zeros((TILES, WIDE, WIDE))
    mode = np.zeros((TILES, WIDE), np.int64)
    for k in range(1, TILES):
        order = SECTORS * a + k
        phase = 2 * np.pi * ((j[:, None] * order[None, :]) % NT) / NT
        tiles[k, :T, :T], tiles[k, :T, T:] = np.cos(phase), np.sin(phase)
        tiles[k, T:, :T], tiles[k, T:, T:] = -np.sin(phase), np.cos(phase)
        mode[k] = np.concatenate([order, order])
    low_cos, low_sin = SECTORS * np.arange(T // 2 + 1), SECTORS * np.arange(1, T // 2)
    mid = SECTORS * np.arange(T // 2) + SECTORS // 2

    def phase_of(order):
        return 2 * np.pi * ((j[:, None] * order[None, :]) % NT) / NT

    tiles[0, :T, :T] = np.concatenate([np.cos(phase_of(low_cos)), np.sin(phase_of(low_sin))], 1)
    tiles[0, T:, T:] = np.concatenate([np.cos(phase_of(mid)), np.sin(phase_of(mid))], 1)
    mode[0] = np.concatenate([low_cos, low_sin, mid, mid])
    mode = np.minimum(mode, NT - mode)
    weight = np.where((mode == 0) | (mode == NT // 2), 1.0, 2.0) / NT
    return tiles, mode.reshape(-1), weight.reshape(-1)


def axial_tables():
    n = np.arange(1, NZ + 1)
    sines = math.sqrt(2.0 / (NZ + 1)) * np.sin(np.pi * ((n[:, None] * n[None, :]) % (2 * (NZ + 1))) / (NZ + 1))
    return sines, 2.0 * np.cos(np.pi * n / (NZ + 1))


C1, C2, C3 = (math.cos(math.pi * n / 8) for n in (1, 2, 3))


def cosine_stage(e):
    f = [e[n] + e[8 - n] for n in range(4)] + [e[4]]
    g = [e[n] - e[8 - n] for n in range(4)]
    outer, inner = f[0] + f[4], f[1] + f[3]
    differ, h = f[0] - f[4], C2 * (f[1] - f[3])
    both = outer + f[2]
    w = C2 * g[2]
    up, down = g[0] + w, g[0] - w
    b, c = C1 * g[1] + C3 * g[3], C3 * g[1] - C1 * g[3]
    return [both + inner, up + b, differ + h, down + c, outer - f[2], down - c, differ - h, up - b, both - inner]


def sine_stage(o):
    u = [None] + [o[n] + o[8 - n] for n in (1, 2, 3)] + [o[4]]
    v = [None] + [o[n] - o[8 - n] for n in (1, 2, 3)]
    h = C2 * (v[1] + v[3])
    w = C2 * u[2]
    up, down = w + u[4], w - u[4]
    b, c = C3 * u[1] + C1 * u[3], C1 * u[1] - C3 * u[3]
    return [None, b + up, h + v[2], c + down, v[1] - v[3], c - down, h - v[2], b - up]


def split(x):
    high = x.astype(BF16)
    return high, (x - high.astype(F32)).astype(BF16)


def product(left, right, dims=((1,), (0,))):
    def one(a, b):
        return lax.dot_general(a, b, (dims, ((), ())), preferred_element_type=F32)

    return one(left[0], right[0]) + (one(left[0], right[1]) + one(left[1], right[0]))


def stacked(ref, rows, half, lanes, right):
    both = lax.dot_general(ref[rows, lanes], right[0], (((1,), (0,)), ((), ())), preferred_element_type=F32)
    high = ref[pl.ds(rows.start, half), lanes]
    return both[:half] + (both[half:] + lax.dot_general(high, right[1], (((1,), (0,)), ((), ())), preferred_element_type=F32))


def kernel(
    azimuth_hbm, radius_hbm, impedance, dens_hbm, swirl_hbm, heat_hbm, ac_hbm, lam_hbm, sines_hbm, pick_hbm, base_hbm, fwd_hbm, bwd_hbm,
    dn, press, acn,
    azimuth, radius, dext, sext, heat, dr, acx, hext, tmask, srcbuf, agbuf, psend, precv, phat,
    send1, recv1, send2, recv2, modes, y, x2, zbuf, inverse, lam, sines, pick, base, fwd, bwd,
    load_sem, halo_s, halo_r, few_s, few_r, f_s, f_r, b_s, b_r,
):
    s, rho = lax.axis_index("sector"), lax.axis_index("radial")
    after, before = lax.rem(s + 1, SECTORS), lax.rem(s + SECTORS - 1, SECTORS)
    inner, outer = lax.rem(rho + RADIALS - 1, RADIALS), lax.rem(rho + 1, RADIALS)
    sine_rest = pl.ds(0, SECTORS - 1)

    def remote(src, dst, send, recv, **where):
        return pltpu.make_async_remote_copy(
            src_ref=src, dst_ref=dst, send_sem=send, recv_sem=recv, device_id=where, device_id_type=pl.DeviceIdType.MESH
        )

    def others(body):
        def step(i, carry):
            body(i)
            return carry

        lax.fori_loop(1, SECTORS, step, 0)

    loads = [
        pltpu.make_async_copy(src, dst, load_sem.at[n])
        for n, (src, dst) in enumerate(
            [
                (dens_hbm, dext.at[pl.ds(R, T * R)]),
                (heat_hbm, heat),
                (swirl_hbm, sext.at[pl.ds(R, T * R)]),
                (azimuth_hbm, azimuth),
                (radius_hbm, radius),
                (sines_hbm, sines),
                (ac_hbm, acx.at[:, pl.ds(8, T)]),
                (lam_hbm, lam),
                (pick_hbm, pick),
                (base_hbm, base),
                (fwd_hbm, fwd),
                (bwd_hbm, bwd),
            ]
        )
    ]
    for load in loads:
        load.start()

    barrier = pltpu.get_barrier_semaphore()

    def greet(i):
        pl.semaphore_signal(barrier, inc=1, device_id={"sector": lax.rem(s + i, SECTORS)}, device_id_type=pl.DeviceIdType.MESH)
        pl.semaphore_signal(barrier, inc=1, device_id={"radial": lax.rem(rho + i, RADIALS)}, device_id_type=pl.DeviceIdType.MESH)

    others(greet)
    loads[0].wait()
    dr[1] = dext[pl.ds(R, T, stride=R), :]
    dr[R] = dext[pl.ds(2 * R - 1, T, stride=R), :]
    pl.semaphore_wait(barrier, 2 * (SECTORS - 1))

    head, tail = pl.ds(0, R), pl.ds(T * R + R, R)
    azimuth_halos = [
        remote(dens_hbm.at[pl.ds(0, R)], dext.at[tail], halo_s.at[0], halo_r.at[0], sector=before),
        remote(dens_hbm.at[pl.ds(T * R - R, R)], dext.at[head], halo_s.at[1], halo_r.at[1], sector=after),
        remote(swirl_hbm.at[pl.ds(0, R)], sext.at[tail], halo_s.at[2], halo_r.at[2], sector=before),
        remote(swirl_hbm.at[pl.ds(T * R - R, R)], sext.at[head], halo_s.at[3], halo_r.at[3], sector=after),
    ]
    wave_halos = [
        remote(ac_hbm.at[:, pl.ds(0, 8)], acx.at[:, pl.ds(T + 8, 8)], halo_s.at[4], halo_r.at[4], sector=before),
        remote(ac_hbm.at[:, pl.ds(T - 8, 8)], acx.at[:, pl.ds(0, 8)], halo_s.at[5], halo_r.at[5], sector=after),
    ]
    to_inner = remote(dr.at[1], dr.at[R + 1], halo_s.at[6], halo_r.at[6], radial=inner)
    to_outer = remote(dr.at[R], dr.at[0], halo_s.at[7], halo_r.at[7], radial=outer)
    for copy in azimuth_halos:
        copy.start()

    @pl.when(rho > 0)
    def _():
        to_inner.start()

    @pl.when(rho < RADIALS - 1)
    def _():
        to_outer.start()

    for copy in wave_halos:
        copy.start()

    loads[1].wait()

    def heat_row(r, total):
        d = dext[pl.ds(R + r, T, stride=R), :]
        dr[r + 1] = d
        return total + heat[pl.ds(r, T, stride=R), :] * d * d

    ends = heat[pl.ds(0, T, stride=R), :] * dr[1] * dr[1] + heat[pl.ds(R - 1, T, stride=R), :] * dr[R] * dr[R]
    hext[8 : 8 + T, :] = lax.fori_loop(1, R - 1, heat_row, ends) * (1.0 / NR)
    heat_halos = [
        remote(hext.at[pl.ds(8, 8)], hext.at[pl.ds(T + 8, 8)], halo_s.at[8], halo_r.at[8], sector=before),
        remote(hext.at[pl.ds(T, 8)], hext.at[pl.ds(0, 8)], halo_s.at[9], halo_r.at[9], sector=after),
    ]
    for copy in heat_halos:
        copy.start()

    for n in (3, 4, 5, 2):
        loads[n].wait()
    theta = lax.broadcasted_iota(jnp.int32, (T, NZ), 0)
    first = azimuth[s]
    tmask[...] = jnp.where((theta >= first) & (theta < first + MOUTH), 1.0, 0.0).astype(F32)
    lane = lax.broadcasted_iota(jnp.int32, (T, NZ), 1)
    for copy in azimuth_halos:
        copy.wait_recv()

    @pl.when(rho > 0)
    def _():
        to_outer.wait_recv()

    @pl.when(rho == 0)
    def _():
        dr[0] = jnp.zeros((T, NZ), F32)

    @pl.when(rho < RADIALS - 1)
    def _():
        to_inner.wait_recv()

    @pl.when(rho == RADIALS - 1)
    def _():
        dr[R + 1] = jnp.zeros((T, NZ), F32)

    sine_pair = (sines[0], sines[1])

    def flow_row(i, carry):
        r = lax.rem(i + R - EDGE, R)
        d = dr[r + 1]
        up = dext[pl.ds(2 * R + r, T, stride=R), :]
        down = dext[pl.ds(r, T, stride=R), :]
        axial = jnp.where(lane < NZ - 1, pltpu.roll(d, NZ - 1, 1), 0.0) + jnp.where(lane > 0, pltpu.roll(d, 1, 1), 0.0)
        laplace = (up + down) + (dr[r] + dr[r + 2]) + axial - 6.0 * d
        flux = sext[pl.ds(2 * R + r, T, stride=R), :] * up - sext[pl.ds(r, T, stride=R), :] * down
        where = rho * R + r - radius[s]
        mouth = jnp.where((where >= 0) & (where < MOUTH), 2.5, 0.0).astype(F32)
        change = 0.05 * laplace - 0.5 * flux + (mouth * tmask[...]) * (1.0 - d)
        dn[pl.ds(r, T, stride=R), :] = d + 0.2 * change
        lines = product(sine_pair, split(change), ((1,), (1,)))
        send1[:, i] = lines.reshape(SECTORS, Q, T)
        return carry

    def flow_chunk(c):
        start, count = SENDS[c]
        lax.fori_loop(start, start + count, flow_row, 0)
        part = pl.ds(start, count)

        def go(i):
            peer = lax.rem(s + i, SECTORS)
            remote(send1.at[peer, part], recv1.at[s, part], f_s.at[c], f_r.at[c], sector=peer).start()

        others(go)
        recv1[s, part] = send1[s, part]

    def forward_all(c):
        part = pl.ds(*SENDS[c])
        return remote(send1.at[sine_rest, part], recv1.at[sine_rest, part], f_s.at[c], f_r.at[c], sector=after)

    def backward_all(c):
        part = pl.ds(*RETURNS[c])
        return remote(send2.at[sine_rest, part], recv2.at[sine_rest, part], b_s.at[c], b_r.at[c], sector=after)

    def tile_rows(peer):
        return pl.ds(pl.multiple_of(8 * peer, 8), 24)

    def share_heat(i):
        peer = lax.rem(rho + i, RADIALS)
        remote(hext.at[tile_rows(peer)], srcbuf.at[rho], few_s.at[0], few_r.at[0], radial=peer).start()

    def share_wave(i):
        peer = lax.rem(rho + i, RADIALS)
        remote(agbuf.at[rho], agbuf.at[rho], few_s.at[1], few_r.at[1], radial=peer).start()

    def share_press(i):
        peer = lax.rem(s + i, SECTORS)
        remote(psend.at[peer], precv.at[s], few_s.at[2], few_r.at[2], sector=peer).start()

    all_heat = remote(srcbuf.at[sine_rest], srcbuf.at[sine_rest], few_s.at[0], few_r.at[0], radial=outer)
    all_wave = remote(agbuf.at[sine_rest], agbuf.at[sine_rest], few_s.at[1], few_r.at[1], radial=outer)
    all_press = remote(psend.at[sine_rest], precv.at[sine_rest], few_s.at[2], few_r.at[2], sector=after)

    flow_chunk(0)

    for copy in heat_halos + wave_halos:
        copy.wait_recv()
    others(share_heat)
    srcbuf[rho] = hext[tile_rows(rho), :]

    flow_chunk(1)

    loads[6].wait()
    all_heat.wait_recv()
    source = srcbuf[0]
    for i in range(1, RADIALS):
        source = source + srcbuf[i]
    source = 0.5 * source
    lane24 = lax.broadcasted_iota(jnp.int32, (24, NZ), 1)
    p, u, w = (acx[n, tile_rows(rho), :] for n in range(3))
    for _ in range(SUBSTEPS):
        u = u - 0.5 * (pltpu.roll(p, 23, 0) - p)
        w = w - 0.5 * (jnp.where(lane24 < NZ - 1, pltpu.roll(p, NZ - 1, 1), 0.0) - p)
        along, axial = u - pltpu.roll(u, 1, 0), w - jnp.where(lane24 > 0, pltpu.roll(w, 1, 1), 0.0)
        p = p - 0.5 * (along + axial) + source
    for n, field in enumerate((p, u, w)):
        agbuf[rho, n] = field[8:16]
    others(share_wave)

    flow_chunk(2)

    all_wave.wait_recv()
    for n in range(3):
        acn[n] = agbuf[:, n].reshape(T, NZ)
    psend[...] = product(sine_pair, split(0.5 * acn[0]), ((1,), (1,))).reshape(SECTORS, Q, T)
    others(share_press)
    precv[s] = psend[s]

    flow_chunk(3)

    for n in (7, 8, 9):
        loads[n].wait()
    whole = impedance[...]
    top = whole.astype(BF16)
    rest = whole - top.astype(F32)
    middle = rest.astype(BF16)
    bottom = (rest - middle.astype(F32)).astype(BF16)

    def diagonal_of(k, carry):
        at = pl.ds(pl.multiple_of(k * WIDE, WIDE), WIDE)
        picked = [
            lax.dot_general(part, pick[0:T, at], (((1,), (0,)), ((), ())), preferred_element_type=F32) for part in (top, middle, bottom)
        ]
        chosen = (picked[0] + picked[1] + picked[2]) * pick[T : T + 2 * Q, at].astype(F32)
        one = 1.0 / (base[0:1, at] + jnp.sum(chosen, axis=0, keepdims=True))
        inverse[0, :, at] = jnp.broadcast_to(one, (Q, WIDE))
        inverse[1, :, at] = jnp.broadcast_to(one * base[1:2, at], (Q, WIDE))
        return carry

    lax.fori_loop(0, TILES, diagonal_of, 0)
    loads[10].wait()

    def keep(row, low, values):
        cosines, odds = values
        for k in range(TILES):
            pair = (cosines[0], cosines[8]) if k == 0 else (cosines[k], odds[k])
            for half, value in enumerate(pair):
                for at, part in zip((row, low), split(value)):
                    y[k, pl.ds(at, 2 * Q), T * half : T * half + T] = part

    def first_stage(x):
        e = [x[0]] + [x[n] + x[SECTORS - n] for n in range(1, 8)] + [x[8]]
        return cosine_stage(e), sine_stage([None] + [x[n] - x[SECTORS - n] for n in range(1, 8)])

    def mode_lanes(k):
        return pl.ds(pl.multiple_of(k * WIDE, WIDE), WIDE)

    def forward_rows(start, count, place, offset, extra):
        total = count + (2 if extra else 0)

        def pair(i, carry):
            x = [recv1[n, pl.ds(start + 2 * i, 2)].reshape(2 * Q, T) for n in range(SECTORS)]
            row = pl.multiple_of(offset + 2 * Q * i, 2 * Q)
            keep(row, pl.multiple_of(row + total * Q, 2 * Q), first_stage(x))
            return carry

        lax.fori_loop(0, count // 2, pair, 0)
        if extra:
            x = [jnp.concatenate([precv[n], precv[n]], 0) for n in range(SECTORS)]
            keep(offset + count * Q, offset + count * Q + total * Q, first_stage(x))

        def tile(k, carry):
            out = stacked(y.at[k], pl.ds(offset, 2 * total * Q), total * Q, pl.ds(0, WIDE), (fwd[0, k], fwd[1, k]))
            for begin, amount, target in place:
                modes[pl.ds(REACH + target, amount), :, mode_lanes(k)] = out[begin * Q : (begin + amount) * Q].reshape(amount, Q, WIDE)
            if extra:
                phat[:, mode_lanes(k)] = out[count * Q : count * Q + Q]
            return carry

        lax.fori_loop(0, TILES, tile, 0)

    modes_inner = remote(modes.at[pl.ds(REACH, REACH)], modes.at[pl.ds(REACH + R, REACH)], halo_s.at[10], halo_r.at[10], radial=inner)
    modes_outer = remote(modes.at[pl.ds(R, REACH)], modes.at[pl.ds(0, REACH)], halo_s.at[11], halo_r.at[11], radial=outer)

    forward_all(0).wait_recv()
    forward_all(1).wait_recv()
    forward_rows(0, 2 * EDGE, ((0, EDGE, R - EDGE), (EDGE, EDGE, 0)), 0, False)

    @pl.when(rho > 0)
    def _():
        modes_inner.start()

    @pl.when(rho < RADIALS - 1)
    def _():
        modes_outer.start()

    axial_sum = lam[pl.ds(pl.multiple_of(s * Q, Q), Q), :]
    keep_low = jnp.where(rho > 0, 1.0, 0.0).astype(F32)
    keep_high = jnp.where(rho < RADIALS - 1, 1.0, 0.0).astype(F32)

    def solve_rows(start, stop, groups):
        rows = range(start - REACH, stop + REACH)

        def block(b, carry):
            at = pl.ds(pl.multiple_of(b * T, T), T)
            inv, last, extra = inverse[0, :, at], inverse[1, :, at], phat[:, at]
            low, high = (inv * keep_low, extra * keep_low), (inv * keep_high, extra * keep_high)
            side = {r: low if r < 0 else high if r >= R else (inv, extra) for r in rows}
            c = {r: modes[r + REACH, :, at] + side[r][1] for r in rows}
            x = {r: c[r] * side[r][0] for r in rows}
            for sweep in range(1, SWEEPS):
                x = {
                    r: ((c[r] + axial_sum * x[r]) + (x[r - 1] + x[r + 1])) * (last if sweep == SWEEPS - 1 else side[r][0])
                    for r in range(start - REACH + sweep, stop + REACH - sweep)
                }
            for begin, amount in groups:
                for n in range(0, amount, 2):
                    row = 2 * begin * Q + n * Q
                    for place, part in zip((row, row + amount * Q), split(jnp.concatenate([x[begin + n], x[begin + n + 1]], 0))):
                        x2[place : place + 2 * Q, at] = part
            return carry

        lax.fori_loop(0, NT // T, block, 0)

    def backward_chunk(c):
        start, count = RETURNS[c]

        def tile(k, carry):
            zbuf[k, pl.ds(start * Q, count * Q), :] = stacked(
                x2, pl.ds(2 * start * Q, 2 * count * Q), count * Q, mode_lanes(k), (bwd[0, k], bwd[1, k])
            )
            return carry

        lax.fori_loop(0, TILES, tile, 0)

        def row(r, carry):
            at = pl.ds(pl.multiple_of(r * Q, Q), Q)
            z = [(zbuf[k, at, 0:T], zbuf[k, at, T:WIDE]) for k in range(TILES)]
            even = cosine_stage([z[0][0]] + [z[k][0] for k in range(1, TILES)] + [z[0][1]])
            odd = sine_stage([None] + [z[k][1] for k in range(1, TILES)])
            send2[0, r], send2[8, r] = even[0], even[8]
            for n in range(1, 8):
                send2[n, r] = even[n] + odd[n]
                send2[SECTORS - n, r] = even[n] - odd[n]
            return carry

        lax.fori_loop(start, start + count, row, 0)
        part = pl.ds(start, count)

        def go(i):
            peer = lax.rem(s + i, SECTORS)
            remote(send2.at[peer, part], recv2.at[s, part], b_s.at[c], b_r.at[c], sector=peer).start()

        others(go)
        recv2[s, part] = send2[s, part]

    forward_all(2).wait_recv()
    all_press.wait_recv()
    forward_rows(2 * EDGE, 4, ((0, 4, 4),), 4 * EDGE * Q, True)

    @pl.when(rho > 0)
    def _():
        modes_outer.wait_recv()

    @pl.when(rho == 0)
    def _():
        modes[0:REACH] = jnp.zeros((REACH, Q, NT), F32)

    solve_rows(0, RETURNS[0][1], RETURNS[:1])
    loads[11].wait()
    backward_chunk(0)

    forward_all(3).wait_recv()
    forward_rows(2 * EDGE + 4, 4, ((0, 4, 8),), 4 * EDGE * Q + 12 * Q, False)

    @pl.when(rho < RADIALS - 1)
    def _():
        modes_inner.wait_recv()

    @pl.when(rho == RADIALS - 1)
    def _():
        modes[REACH + R : R + 2 * REACH] = jnp.zeros((REACH, Q, NT), F32)

    solve_rows(RETURNS[0][1], R, RETURNS[1:])
    for c in range(1, len(RETURNS)):
        backward_chunk(c)

    for copy in azimuth_halos + wave_halos + heat_halos + [all_heat, all_wave, all_press] + [forward_all(c) for c in range(len(SENDS))]:
        copy.wait_send()

    @pl.when(rho > 0)
    def _():
        to_inner.wait_send()
        modes_inner.wait_send()

    @pl.when(rho < RADIALS - 1)
    def _():
        to_outer.wait_send()
        modes_outer.wait_send()

    def finish(r, carry):
        lines = recv2[:, r].reshape(NZ, T).T
        press[pl.ds(r, T, stride=R), :] = product(split(lines), sine_pair)
        return carry

    for c, (start, count) in enumerate(RETURNS):
        backward_all(c).wait_recv()
        lax.fori_loop(start, start + count, finish, 0)
    for c in range(len(RETURNS)):
        backward_all(c).wait_send()


def shards(density, swirl, heat_rate, acoustic, mode_impedance, mouth_azimuth, mouth_radius):
    tiles, mode, weight = mode_tables()
    sines, axial_sum = axial_tables()
    impedance = jnp.pad(mode_impedance, (0, 2 * Q * T - mode_impedance.shape[0])).reshape(2 * Q, T)
    pick = np.concatenate([np.arange(T)[:, None] == mode[None, :] % T, np.arange(2 * Q)[:, None] == mode[None, :] // T]).astype(BF16)
    base = np.stack([4.0 + 2.0 - 2.0 * np.cos(2 * np.pi * mode / NT), weight]).astype(np.float32)
    base = np.concatenate([base, np.zeros((6, NT), np.float32)])
    lam = np.repeat(axial_sum[:, None], T, 1).astype(np.float32)
    flat = lambda x: x.reshape(T * R, NZ)
    pinned = lambda x: pltpu.with_memory_space_constraint(jnp.asarray(x), pltpu.HBM)
    vmem, anywhere = pl.BlockSpec(memory_space=pltpu.VMEM), pl.BlockSpec(memory_space=pltpu.HBM)
    dma = pltpu.SemaphoreType.DMA
    fields = [density, swirl, heat_rate]
    dn, press, acn = pl.pallas_call(
        kernel,
        out_shape=(
            jax.ShapeDtypeStruct((T * R, NZ), F32),
            jax.ShapeDtypeStruct((T * R, NZ), F32),
            jax.ShapeDtypeStruct((3, T, NZ), F32),
        ),
        in_specs=[anywhere] * 2 + [vmem] + [anywhere] * 10,
        out_specs=(vmem, vmem, vmem),
        scratch_shapes=[
            pltpu.SMEM((BURNERS,), jnp.int32),
            pltpu.SMEM((BURNERS,), jnp.int32),
            pltpu.VMEM(((T + 2) * R, NZ), F32),
            pltpu.VMEM(((T + 2) * R, NZ), F32),
            pltpu.VMEM((T * R, NZ), F32),
            pltpu.VMEM((R + 2, T, NZ), F32),
            pltpu.VMEM((3, T + 16, NZ), F32),
            pltpu.VMEM((T + 16, NZ), F32),
            pltpu.VMEM((T, NZ), F32),
            pltpu.VMEM((RADIALS, 24, NZ), F32),
            pltpu.VMEM((RADIALS, 3, 8, NZ), F32),
            pltpu.VMEM((SECTORS, Q, T), F32),
            pltpu.VMEM((SECTORS, Q, T), F32),
            pltpu.VMEM((Q, NT), F32),
            pltpu.VMEM((SECTORS, R, Q, T), F32),
            pltpu.VMEM((SECTORS, R, Q, T), F32),
            pltpu.VMEM((SECTORS, R, Q, T), F32),
            pltpu.VMEM((SECTORS, R, Q, T), F32),
            pltpu.VMEM((R + 2 * REACH, Q, NT), F32),
            pltpu.VMEM((TILES, 2 * (R + 2) * Q, WIDE), BF16),
            pltpu.VMEM((2 * R * Q, NT), BF16),
            pltpu.VMEM((TILES, R * Q, WIDE), F32),
            pltpu.VMEM((2, Q, NT), F32),
            pltpu.VMEM((NZ, T), F32),
            pltpu.VMEM((2, NZ, NZ), BF16),
            pltpu.VMEM((T + 2 * Q, NT), BF16),
            pltpu.VMEM((8, NT), F32),
            pltpu.VMEM((2, TILES, WIDE, WIDE), BF16),
            pltpu.VMEM((2, TILES, WIDE, WIDE), BF16),
            dma((12,)),
            dma((12,)),
            dma((12,)),
            dma((3,)),
            dma((3,)),
            dma((len(SENDS),)),
            dma((len(SENDS),)),
            dma((len(RETURNS),)),
            dma((len(RETURNS),)),
        ],
        compiler_params=pltpu.CompilerParams(collective_id=0, has_side_effects=True, vmem_limit_bytes=VMEM_LIMIT),
    )(
        pinned(mouth_azimuth), pinned(mouth_radius), impedance, *[pinned(flat(x)) for x in fields], pinned(acoustic), pinned(lam),
        pinned(halves(sines)), pinned(pick), pinned(base), pinned(halves(tiles)), pinned(halves(tiles.transpose(0, 2, 1))),
    )
    return dn.reshape(T, R, NZ), press.reshape(T, R, NZ), acn


def solution(mesh):
    cells, columns = P("sector", "radial", None), P(None, "sector", None)
    return jax.shard_map(
        shards,
        mesh=mesh,
        in_specs=(cells, cells, cells, columns, P(), P(), P()),
        out_specs=(cells, cells, columns),
        check_vma=False,
    )
```

time: 96.8 us -> 74 us (0.76); the launches traced: 95.3 us -> 73.7 us
  Pallas kernels: 81.1 us -> 69.8 us
  local copies, waits for them, and re-layouts: 12 us -> 3.32 us
  other arithmetic: 1.51 us -> 0 us
    pallas_call x1, Pallas kernels: 81.1 us -> 69.8 us  [shards(): pl.pallas_call(kernel, out_shape=(jax.ShapeDtypeStruct((T * R, NZ), F32),...]
    unnamed x21 -> x3, local copies, waits for them, and re-layouts: 10.4 us -> 2.62 us
    slice x5 -> x0, local copies, waits for them, and re-layouts: 1.53 us -> none  [the longest x1 0.76 us: shards(): mode_impedance[1:half][::-1]]
where the time goes in v2:
time: 74 us; the launch traced here: 73.7 us
  Pallas kernels  69.8 us (94%)
  local copies, waits for them, and re-layouts  3.32 us (4%)
    pallas_call x1, Pallas kernels, shards(): pl.pallas_call(kernel, out_shape=(jax.ShapeDtypeStruct((T * R, NZ), F32),...  69.8 us
    unnamed x3, local copies, waits for them, and re-layouts  2.62 us

profile of v2, /device:TPU:8, one launch (start us, length us, event | category | flops | bytes accessed | tf_op | source)
XLA Modules:
  0.0 73.7 jit_solution(4631714962554347194)
XLA Ops:
  0.6 0.7 pad_bitcast_fusion.impedance
  1.3 69.8 %shard_map.148 = (f32[2048,128]{1,0:T(8,128)S(1)}, f32[2048,128]{1,0:T(8,128)S(1)}, f32[3,128,128]{2,1,0:T(8,128)S(1)}) custom-call(s32[16]{0:T(128)} %azimuth_hbm.1, s32[16]{0:T(128)} %radius_hbm.1, f32[16,128]{1,0:T(8,128)S(1)} %pad_bitcast_fusion.impedance, f32[2048,128]{1,0:T(8,128)} %bitcast.9, f32[2048,128]{1,0:T(8,128)} %bitcast.10, ...), custom_call_target="tpu_custom_call" | custom-call | tf_op jit(solution)/shard_map/pallas_call | solution.py:536
  71.1 1.0 %copy.19 = f32[128,16,128]{2,1,0:T(8,128)} copy(f32[128,16,128]{2,1,0:T(8,128)S(1)} %bitcast.8) | data formatting | bytes 2097152
  72.1 1.0 %copy.20 = f32[128,16,128]{2,1,0:T(8,128)} copy(f32[128,16,128]{2,1,0:T(8,128)S(1)} %bitcast.7) | data formatting | bytes 2097152
  73.1 0.7 copy.21

commit v3 on v2

--- a/solution.py
+++ b/solution.py
@@ -21,8 +21,11 @@
 WIDE = 2 * T
 BURNERS = 16
 EDGE = 4
-SENDS = ((0, 4), (4, 4), (8, 4), (12, 4))
+SENDS = ((0, 1), (1, 3), (4, 4), (8, 4), (12, 4))
 RETURNS = ((0, 4), (4, 6), (10, 4), (14, 2))
+Y_MIDDLE = 4 * EDGE * Q
+EDGE_SENDS, MIDDLE = 3, 4
+REST = R - 2 * EDGE - MIDDLE
 VMEM_LIMIT = 48 * 2**20
 
 F32, BF16 = jnp.float32, jnp.bfloat16
@@ -118,7 +121,7 @@
     s, rho = lax.axis_index("sector"), lax.axis_index("radial")
     after, before = lax.rem(s + 1, SECTORS), lax.rem(s + SECTORS - 1, SECTORS)
     inner, outer = lax.rem(rho + RADIALS - 1, RADIALS), lax.rem(rho + 1, RADIALS)
-    sine_rest = pl.ds(0, SECTORS - 1)
+    all_but_one = pl.ds(0, SECTORS - 1)
 
     def remote(src, dst, send, recv, **where):
         return pltpu.make_async_remote_copy(
@@ -151,9 +154,6 @@
             ]
         )
     ]
-    for load in loads:
-        load.start()
-
     barrier = pltpu.get_barrier_semaphore()
 
     def greet(i):
@@ -161,9 +161,8 @@
         pl.semaphore_signal(barrier, inc=1, device_id={"radial": lax.rem(rho + i, RADIALS)}, device_id_type=pl.DeviceIdType.MESH)
 
     others(greet)
-    loads[0].wait()
-    dr[1] = dext[pl.ds(R, T, stride=R), :]
-    dr[R] = dext[pl.ds(2 * R - 1, T, stride=R), :]
+    for load in loads[:7]:
+        load.start()
     pl.semaphore_wait(barrier, 2 * (SECTORS - 1))
 
     head, tail = pl.ds(0, R), pl.ds(T * R + R, R)
@@ -181,6 +180,9 @@
     to_outer = remote(dr.at[R], dr.at[0], halo_s.at[7], halo_r.at[7], radial=outer)
     for copy in azimuth_halos:
         copy.start()
+    loads[0].wait()
+    dr[1] = dext[pl.ds(R, T, stride=R), :]
+    dr[R] = dext[pl.ds(2 * R - 1, T, stride=R), :]
 
     @pl.when(rho > 0)
     def _():
@@ -192,7 +194,6 @@
 
     for copy in wave_halos:
         copy.start()
-
     loads[1].wait()
 
     def heat_row(r, total):
@@ -208,6 +209,8 @@
     ]
     for copy in heat_halos:
         copy.start()
+    for load in loads[7:]:
+        load.start()
 
     for n in (3, 4, 5, 2):
         loads[n].wait()
@@ -217,22 +220,6 @@
     lane = lax.broadcasted_iota(jnp.int32, (T, NZ), 1)
     for copy in azimuth_halos:
         copy.wait_recv()
-
-    @pl.when(rho > 0)
-    def _():
-        to_outer.wait_recv()
-
-    @pl.when(rho == 0)
-    def _():
-        dr[0] = jnp.zeros((T, NZ), F32)
-
-    @pl.when(rho < RADIALS - 1)
-    def _():
-        to_inner.wait_recv()
-
-    @pl.when(rho == RADIALS - 1)
-    def _():
-        dr[R + 1] = jnp.zeros((T, NZ), F32)
 
     sine_pair = (sines[0], sines[1])
 
@@ -266,11 +253,11 @@
 
     def forward_all(c):
         part = pl.ds(*SENDS[c])
-        return remote(send1.at[sine_rest, part], recv1.at[sine_rest, part], f_s.at[c], f_r.at[c], sector=after)
+        return remote(send1.at[all_but_one, part], recv1.at[all_but_one, part], f_s.at[c], f_r.at[c], sector=after)
 
     def backward_all(c):
         part = pl.ds(*RETURNS[c])
-        return remote(send2.at[sine_rest, part], recv2.at[sine_rest, part], b_s.at[c], b_r.at[c], sector=after)
+        return remote(send2.at[all_but_one, part], recv2.at[all_but_one, part], b_s.at[c], b_r.at[c], sector=after)
 
     def tile_rows(peer):
         return pl.ds(pl.multiple_of(8 * peer, 8), 24)
@@ -287,18 +274,35 @@
         peer = lax.rem(s + i, SECTORS)
         remote(psend.at[peer], precv.at[s], few_s.at[2], few_r.at[2], sector=peer).start()
 
-    all_heat = remote(srcbuf.at[sine_rest], srcbuf.at[sine_rest], few_s.at[0], few_r.at[0], radial=outer)
-    all_wave = remote(agbuf.at[sine_rest], agbuf.at[sine_rest], few_s.at[1], few_r.at[1], radial=outer)
-    all_press = remote(psend.at[sine_rest], precv.at[sine_rest], few_s.at[2], few_r.at[2], sector=after)
+    all_heat = remote(srcbuf.at[all_but_one], srcbuf.at[all_but_one], few_s.at[0], few_r.at[0], radial=outer)
+    all_wave = remote(agbuf.at[all_but_one], agbuf.at[all_but_one], few_s.at[1], few_r.at[1], radial=outer)
+    all_press = remote(psend.at[all_but_one], precv.at[all_but_one], few_s.at[2], few_r.at[2], sector=after)
 
     flow_chunk(0)
+
+    @pl.when(rho > 0)
+    def _():
+        to_outer.wait_recv()
+
+    @pl.when(rho == 0)
+    def _():
+        dr[0] = jnp.zeros((T, NZ), F32)
+
+    @pl.when(rho < RADIALS - 1)
+    def _():
+        to_inner.wait_recv()
+
+    @pl.when(rho == RADIALS - 1)
+    def _():
+        dr[R + 1] = jnp.zeros((T, NZ), F32)
 
     for copy in heat_halos + wave_halos:
         copy.wait_recv()
     others(share_heat)
     srcbuf[rho] = hext[tile_rows(rho), :]
 
-    flow_chunk(1)
+    for c in range(1, EDGE_SENDS):
+        flow_chunk(c)
 
     loads[6].wait()
     all_heat.wait_recv()
@@ -317,7 +321,7 @@
         agbuf[rho, n] = field[8:16]
     others(share_wave)
 
-    flow_chunk(2)
+    flow_chunk(EDGE_SENDS)
 
     all_wave.wait_recv()
     for n in range(3):
@@ -326,7 +330,7 @@
     others(share_press)
     precv[s] = psend[s]
 
-    flow_chunk(3)
+    flow_chunk(EDGE_SENDS + 1)
 
     for n in (7, 8, 9):
         loads[n].wait()
@@ -387,13 +391,13 @@
                 phat[:, mode_lanes(k)] = out[count * Q : count * Q + Q]
             return carry
 
-        lax.fori_loop(0, TILES, tile, 0)
+        lax.fori_loop(0, TILES, tile, 0, unroll=True)
 
     modes_inner = remote(modes.at[pl.ds(REACH, REACH)], modes.at[pl.ds(REACH + R, REACH)], halo_s.at[10], halo_r.at[10], radial=inner)
     modes_outer = remote(modes.at[pl.ds(R, REACH)], modes.at[pl.ds(0, REACH)], halo_s.at[11], halo_r.at[11], radial=outer)
 
-    forward_all(0).wait_recv()
-    forward_all(1).wait_recv()
+    for c in range(EDGE_SENDS):
+        forward_all(c).wait_recv()
     forward_rows(0, 2 * EDGE, ((0, EDGE, R - EDGE), (EDGE, EDGE, 0)), 0, False)
 
     @pl.when(rho > 0)
@@ -441,7 +445,7 @@
             )
             return carry
 
-        lax.fori_loop(0, TILES, tile, 0)
+        lax.fori_loop(0, TILES, tile, 0, unroll=True)
 
         def row(r, carry):
             at = pl.ds(pl.multiple_of(r * Q, Q), Q)
@@ -464,9 +468,9 @@
         others(go)
         recv2[s, part] = send2[s, part]
 
-    forward_all(2).wait_recv()
+    forward_all(EDGE_SENDS).wait_recv()
     all_press.wait_recv()
-    forward_rows(2 * EDGE, 4, ((0, 4, 4),), 4 * EDGE * Q, True)
+    forward_rows(2 * EDGE, MIDDLE, ((0, MIDDLE, EDGE),), Y_MIDDLE, True)
 
     @pl.when(rho > 0)
     def _():
@@ -480,8 +484,8 @@
     loads[11].wait()
     backward_chunk(0)
 
-    forward_all(3).wait_recv()
-    forward_rows(2 * EDGE + 4, 4, ((0, 4, 8),), 4 * EDGE * Q + 12 * Q, False)
+    forward_all(EDGE_SENDS + 1).wait_recv()
+    forward_rows(2 * EDGE + MIDDLE, REST, ((0, REST, EDGE + MIDDLE),), Y_MIDDLE + 2 * (MIDDLE + 2) * Q, False)
 
     @pl.when(rho < RADIALS - 1)
     def _():
@@ -518,6 +522,14 @@
         lax.fori_loop(start, start + count, finish, 0)
     for c in range(len(RETURNS)):
         backward_all(c).wait_send()
+
+
+def deliver(dn, press, acn, dn_hbm, press_hbm, acn_hbm, sem):
+    copies = [pltpu.make_async_copy(*pair, sem.at[n]) for n, pair in enumerate(((dn, dn_hbm), (press, press_hbm), (acn, acn_hbm)))]
+    for copy in copies:
+        copy.start()
+    for copy in copies:
+        copy.wait()
 
 
 def shards(density, swirl, heat_rate, acoustic, mode_impedance, mouth_azimuth, mouth_radius):
@@ -587,6 +599,15 @@
         pinned(mouth_azimuth), pinned(mouth_radius), impedance, *[pinned(flat(x)) for x in fields], pinned(acoustic), pinned(lam),
         pinned(halves(sines)), pinned(pick), pinned(base), pinned(halves(tiles)), pinned(halves(tiles.transpose(0, 2, 1))),
     )
+    results = (dn, press, acn)
+    dn, press, acn = pl.pallas_call(
+        deliver,
+        out_shape=tuple(jax.ShapeDtypeStruct(x.shape, F32) for x in results),
+        in_specs=[vmem] * 3,
+        out_specs=(anywhere,) * 3,
+        scratch_shapes=[dma((3,))],
+        compiler_params=pltpu.CompilerParams(vmem_limit_bytes=2**20),
+    )(*results)
     return dn.reshape(T, R, NZ), press.reshape(T, R, NZ), acn
 
 

time: 74 us -> 69.1 us (0.934)
  local copies, waits for them, and re-layouts: 3.32 us -> 0.7 us
  Pallas kernels: 69.8 us -> 67.6 us
    pallas_call x1, Pallas kernels: 69.8 us -> 66.2 us  [shards(): pl.pallas_call(kernel, out_shape=(jax.ShapeDtypeStruct((T * R, NZ), F32),...]
    unnamed x3 -> x0, local copies, waits for them, and re-layouts: 2.62 us -> none
    pallas_call x0 -> x1, Pallas kernels: none -> 1.4 us  [shards(): pl.pallas_call(deliver, out_shape=tuple((jax.ShapeDtypeStruct(x.shape, F3...]
where the time goes in v3:
time: 69.1 us; the launch traced here: 69 us
  Pallas kernels  67.6 us (98%)
  local copies, waits for them, and re-layouts  0.7 us (1%)
    pallas_call x1, Pallas kernels, shards(): pl.pallas_call(kernel, out_shape=(jax.ShapeDtypeStruct((T * R, NZ), F32),...  66.2 us
    pallas_call x1, Pallas kernels, shards(): pl.pallas_call(deliver, out_shape=tuple((jax.ShapeDtypeStruct(x.shape, F3...  1.4 us

profile of v3, /device:TPU:8, one launch (start us, length us, event | category | flops | bytes accessed | tf_op | source)
XLA Modules:
  0.0 69.0 jit_solution(14192060779495129911)
XLA Ops:
  0.6 0.7 %pad_bitcast_fusion.impedance = f32[16,128]{1,0:T(8,128)S(1)} fusion(f32[1025]{0:T(1024)} %param.17), kind=kLoop, calls=%fused_computation | loop fusion | bytes 12292 | tf_op jit(solution)/shard_map/reshape | solution.py:538
  1.3 66.2 %shard_map.148 = (f32[2048,128]{1,0:T(8,128)S(1)}, f32[2048,128]{1,0:T(8,128)S(1)}, f32[3,128,128]{2,1,0:T(8,128)S(1)}) custom-call(s32[16]{0:T(128)} %azimuth_hbm.1, s32[16]{0:T(128)} %radius_hbm.1, f32[16,128]{1,0:T(8,128)S(1)} %pad_bitcast_fusion.impedance, f32[2048,128]{1,0:T(8,128)} %bitcast.7, f32[2048,128]{1,0:T(8,128)} %bitcast.8, ...), custom_call_target="tpu_custom_call" | custom-call | tf_op jit(solution)/shard_map/pallas_call | solution.py:548
  67.6 1.4 %shard_map.149 = (f32[2048,128]{1,0:T(8,128)}, f32[2048,128]{1,0:T(8,128)}, f32[3,128,128]{2,1,0:T(8,128)}) custom-call(f32[2048,128]{1,0:T(8,128)S(1)} %get-tuple-element.9.dn, f32[2048,128]{1,0:T(8,128)S(1)} %get-tuple-element.10.press, f32[3,128,128]{2,1,0:T(8,128)S(1)} %get-tuple-element.11.acn), custom_call_target="tpu_custom_call" | custom-call | tf_op jit(solution)/shard_map/pallas_call | solution.py:603

commit v4 on v3

--- a/solution.py
+++ b/solution.py
@@ -22,7 +22,7 @@
 BURNERS = 16
 EDGE = 4
 SENDS = ((0, 1), (1, 3), (4, 4), (8, 4), (12, 4))
-RETURNS = ((0, 4), (4, 6), (10, 4), (14, 2))
+RETURNS = ((0, 4), (4, 4), (8, 6), (14, 2))
 Y_MIDDLE = 4 * EDGE * Q
 EDGE_SENDS, MIDDLE = 3, 4
 REST = R - 2 * EDGE - MIDDLE
@@ -112,9 +112,9 @@
 
 
 def kernel(
-    azimuth_hbm, radius_hbm, impedance, dens_hbm, swirl_hbm, heat_hbm, ac_hbm, lam_hbm, sines_hbm, pick_hbm, base_hbm, fwd_hbm, bwd_hbm,
+    azimuth_hbm, radius_hbm, impedance_hbm, dens_hbm, swirl_hbm, heat_hbm, ac_hbm, lam_hbm, sines_hbm, pick_hbm, base_hbm, fwd_hbm, bwd_hbm,
     dn, press, acn,
-    azimuth, radius, dext, sext, heat, dr, acx, hext, tmask, srcbuf, agbuf, psend, precv, phat,
+    azimuth, radius, impedance, topmost, dext, sext, heat, dr, acx, hext, tmask, srcbuf, agbuf, psend, precv, phat,
     send1, recv1, send2, recv2, modes, y, x2, zbuf, inverse, lam, sines, pick, base, fwd, bwd,
     load_sem, halo_s, halo_r, few_s, few_r, f_s, f_r, b_s, b_r,
 ):
@@ -135,13 +135,14 @@
 
         lax.fori_loop(1, SECTORS, step, 0)
 
+    low, inside, high = pl.ds(0, R), pl.ds(R, (T - 2) * R), pl.ds(T * R - R, R)
     loads = [
         pltpu.make_async_copy(src, dst, load_sem.at[n])
         for n, (src, dst) in enumerate(
             [
-                (dens_hbm, dext.at[pl.ds(R, T * R)]),
+                (dens_hbm.at[inside], dext.at[pl.ds(2 * R, (T - 2) * R)]),
                 (heat_hbm, heat),
-                (swirl_hbm, sext.at[pl.ds(R, T * R)]),
+                (swirl_hbm.at[inside], sext.at[pl.ds(2 * R, (T - 2) * R)]),
                 (azimuth_hbm, azimuth),
                 (radius_hbm, radius),
                 (sines_hbm, sines),
@@ -151,6 +152,12 @@
                 (base_hbm, base),
                 (fwd_hbm, fwd),
                 (bwd_hbm, bwd),
+                (impedance_hbm, impedance),
+                (impedance_hbm, topmost),
+                (dens_hbm.at[low], dext.at[pl.ds(R, R)]),
+                (dens_hbm.at[high], dext.at[pl.ds(T * R, R)]),
+                (swirl_hbm.at[low], sext.at[pl.ds(R, R)]),
+                (swirl_hbm.at[high], sext.at[pl.ds(T * R, R)]),
             ]
         )
     ]
@@ -161,16 +168,16 @@
         pl.semaphore_signal(barrier, inc=1, device_id={"radial": lax.rem(rho + i, RADIALS)}, device_id_type=pl.DeviceIdType.MESH)
 
     others(greet)
-    for load in loads[:7]:
+    for load in loads[14:] + loads[:7]:
         load.start()
     pl.semaphore_wait(barrier, 2 * (SECTORS - 1))
 
     head, tail = pl.ds(0, R), pl.ds(T * R + R, R)
     azimuth_halos = [
-        remote(dens_hbm.at[pl.ds(0, R)], dext.at[tail], halo_s.at[0], halo_r.at[0], sector=before),
-        remote(dens_hbm.at[pl.ds(T * R - R, R)], dext.at[head], halo_s.at[1], halo_r.at[1], sector=after),
-        remote(swirl_hbm.at[pl.ds(0, R)], sext.at[tail], halo_s.at[2], halo_r.at[2], sector=before),
-        remote(swirl_hbm.at[pl.ds(T * R - R, R)], sext.at[head], halo_s.at[3], halo_r.at[3], sector=after),
+        remote(dext.at[pl.ds(R, R)], dext.at[tail], halo_s.at[0], halo_r.at[0], sector=before),
+        remote(dext.at[pl.ds(T * R, R)], dext.at[head], halo_s.at[1], halo_r.at[1], sector=after),
+        remote(sext.at[pl.ds(R, R)], sext.at[tail], halo_s.at[2], halo_r.at[2], sector=before),
+        remote(sext.at[pl.ds(T * R, R)], sext.at[head], halo_s.at[3], halo_r.at[3], sector=after),
     ]
     wave_halos = [
         remote(ac_hbm.at[:, pl.ds(0, 8)], acx.at[:, pl.ds(T + 8, 8)], halo_s.at[4], halo_r.at[4], sector=before),
@@ -178,6 +185,8 @@
     ]
     to_inner = remote(dr.at[1], dr.at[R + 1], halo_s.at[6], halo_r.at[6], radial=inner)
     to_outer = remote(dr.at[R], dr.at[0], halo_s.at[7], halo_r.at[7], radial=outer)
+    for load in loads[14:]:
+        load.wait()
     for copy in azimuth_halos:
         copy.start()
     loads[0].wait()
@@ -209,7 +218,7 @@
     ]
     for copy in heat_halos:
         copy.start()
-    for load in loads[7:]:
+    for load in loads[7:14]:
         load.start()
 
     for n in (3, 4, 5, 2):
@@ -332,9 +341,9 @@
 
     flow_chunk(EDGE_SENDS + 1)
 
-    for n in (7, 8, 9):
+    for n in (7, 8, 9, 12, 13):
         loads[n].wait()
-    whole = impedance[...]
+    whole = jnp.concatenate([impedance[0 : NT // 2].reshape(Q, T), jnp.full((Q, T), topmost[NT // 2], F32)], 0)
     top = whole.astype(BF16)
     rest = whole - top.astype(F32)
     middle = rest.astype(BF16)
@@ -495,8 +504,9 @@
     def _():
         modes[REACH + R : R + 2 * REACH] = jnp.zeros((REACH, Q, NT), F32)
 
-    solve_rows(RETURNS[0][1], R, RETURNS[1:])
     for c in range(1, len(RETURNS)):
+        start, count = RETURNS[c]
+        solve_rows(start, start + count, RETURNS[c : c + 1])
         backward_chunk(c)
 
     for copy in azimuth_halos + wave_halos + heat_halos + [all_heat, all_wave, all_press] + [forward_all(c) for c in range(len(SENDS))]:
@@ -519,7 +529,7 @@
 
     for c, (start, count) in enumerate(RETURNS):
         backward_all(c).wait_recv()
-        lax.fori_loop(start, start + count, finish, 0)
+        lax.fori_loop(start, start + count, finish, 0, unroll=2)
     for c in range(len(RETURNS)):
         backward_all(c).wait_send()
 
@@ -535,7 +545,6 @@
 def shards(density, swirl, heat_rate, acoustic, mode_impedance, mouth_azimuth, mouth_radius):
     tiles, mode, weight = mode_tables()
     sines, axial_sum = axial_tables()
-    impedance = jnp.pad(mode_impedance, (0, 2 * Q * T - mode_impedance.shape[0])).reshape(2 * Q, T)
     pick = np.concatenate([np.arange(T)[:, None] == mode[None, :] % T, np.arange(2 * Q)[:, None] == mode[None, :] // T]).astype(BF16)
     base = np.stack([4.0 + 2.0 - 2.0 * np.cos(2 * np.pi * mode / NT), weight]).astype(np.float32)
     base = np.concatenate([base, np.zeros((6, NT), np.float32)])
@@ -552,11 +561,13 @@
             jax.ShapeDtypeStruct((T * R, NZ), F32),
             jax.ShapeDtypeStruct((3, T, NZ), F32),
         ),
-        in_specs=[anywhere] * 2 + [vmem] + [anywhere] * 10,
+        in_specs=[anywhere] * 13,
         out_specs=(vmem, vmem, vmem),
         scratch_shapes=[
             pltpu.SMEM((BURNERS,), jnp.int32),
             pltpu.SMEM((BURNERS,), jnp.int32),
+            pltpu.VMEM((NT // 2 + 1,), F32),
+            pltpu.SMEM((NT // 2 + 1,), F32),
             pltpu.VMEM(((T + 2) * R, NZ), F32),
             pltpu.VMEM(((T + 2) * R, NZ), F32),
             pltpu.VMEM((T * R, NZ), F32),
@@ -584,7 +595,7 @@
             pltpu.VMEM((8, NT), F32),
             pltpu.VMEM((2, TILES, WIDE, WIDE), BF16),
             pltpu.VMEM((2, TILES, WIDE, WIDE), BF16),
-            dma((12,)),
+            dma((18,)),
             dma((12,)),
             dma((12,)),
             dma((3,)),
@@ -596,7 +607,7 @@
         ],
         compiler_params=pltpu.CompilerParams(collective_id=0, has_side_effects=True, vmem_limit_bytes=VMEM_LIMIT),
     )(
-        pinned(mouth_azimuth), pinned(mouth_radius), impedance, *[pinned(flat(x)) for x in fields], pinned(acoustic), pinned(lam),
+        pinned(mouth_azimuth), pinned(mouth_radius), pinned(mode_impedance), *[pinned(flat(x)) for x in fields], pinned(acoustic), pinned(lam),
         pinned(halves(sines)), pinned(pick), pinned(base), pinned(halves(tiles)), pinned(halves(tiles.transpose(0, 2, 1))),
     )
     results = (dn, press, acn)

time: 69.1 us -> 67.8 us (0.981)
  local copies, waits for them, and re-layouts: 0.7 us -> 0 us
    reshape x1 -> x0, local copies, waits for them, and re-layouts: 0.7 us -> none  [shards(): jnp.pad(mode_impedance, (0, 2 * Q * T - mode_impedance.shape[0]))]
where the time goes in v4:
time: 67.8 us
  Pallas kernels  67.1 us (99%)
    pallas_call x1, Pallas kernels, shards(): pl.pallas_call(kernel, out_shape=(jax.ShapeDtypeStruct((T * R, NZ), F32),...  65.7 us
    pallas_call x1, Pallas kernels, shards(): pl.pallas_call(deliver, out_shape=tuple((jax.ShapeDtypeStruct(x.shape, F3...  1.4 us

profile of v4, /device:TPU:8, one launch (start us, length us, event | category | flops | bytes accessed | tf_op | source)
XLA Modules:
  0.0 67.8 jit_solution(6803639582155371341)
XLA Ops:
  0.6 65.7 %shard_map.148 = (f32[2048,128]{1,0:T(8,128)S(1)}, f32[2048,128]{1,0:T(8,128)S(1)}, f32[3,128,128]{2,1,0:T(8,128)S(1)}) custom-call(s32[16]{0:T(128)} %azimuth_hbm.1, s32[16]{0:T(128)} %radius_hbm.1, f32[1025]{0:T(1024)} %impedance_hbm.1, f32[2048,128]{1,0:T(8,128)} %bitcast.5, f32[2048,128]{1,0:T(8,128)} %bitcast.6, f32[2048,128]{1,0:T(8,128)} %bitcast.7, ...), custom_call_target="tpu_custom_call" | custom-call | tf_op jit(solution)/shard_map/pallas_call | solution.py:557
  66.4 1.4 %shard_map.149 = (f32[2048,128]{1,0:T(8,128)}, f32[2048,128]{1,0:T(8,128)}, f32[3,128,128]{2,1,0:T(8,128)}) custom-call(f32[2048,128]{1,0:T(8,128)S(1)} %get-tuple-element.9.dn, f32[2048,128]{1,0:T(8,128)S(1)} %get-tuple-element.10.press, f32[3,128,128]{2,1,0:T(8,128)S(1)} %get-tuple-element.11.acn), custom_call_target="tpu_custom_call" | custom-call | tf_op jit(solution)/shard_map/pallas_call | solution.py:614

commit v5 on v4

--- a/solution.py
+++ b/solution.py
@@ -211,7 +211,7 @@
         return total + heat[pl.ds(r, T, stride=R), :] * d * d
 
     ends = heat[pl.ds(0, T, stride=R), :] * dr[1] * dr[1] + heat[pl.ds(R - 1, T, stride=R), :] * dr[R] * dr[R]
-    hext[8 : 8 + T, :] = lax.fori_loop(1, R - 1, heat_row, ends) * (1.0 / NR)
+    hext[8 : 8 + T, :] = lax.fori_loop(1, R - 1, heat_row, ends, unroll=2) * (1.0 / NR)
     heat_halos = [
         remote(hext.at[pl.ds(8, 8)], hext.at[pl.ds(T + 8, 8)], halo_s.at[8], halo_r.at[8], sector=before),
         remote(hext.at[pl.ds(T, 8)], hext.at[pl.ds(0, 8)], halo_s.at[9], halo_r.at[9], sector=after),
@@ -360,7 +360,7 @@
         inverse[1, :, at] = jnp.broadcast_to(one * base[1:2, at], (Q, WIDE))
         return carry
 
-    lax.fori_loop(0, TILES, diagonal_of, 0)
+    lax.fori_loop(0, TILES, diagonal_of, 0, unroll=2)
     loads[10].wait()
 
     def keep(row, low, values):
@@ -467,7 +467,7 @@
                 send2[SECTORS - n, r] = even[n] - odd[n]
             return carry
 
-        lax.fori_loop(start, start + count, row, 0)
+        lax.fori_loop(start, start + count, row, 0, unroll=2)
         part = pl.ds(start, count)
 
         def go(i):

time: 67.8 us -> 67.4 us (level)
  no operation moved by 1% of the time
where the time goes in v5:
time: 67.4 us; the launch traced here: 67.3 us
  Pallas kernels  66.7 us (99%)
    pallas_call x1, Pallas kernels, shards(): pl.pallas_call(kernel, out_shape=(jax.ShapeDtypeStruct((T * R, NZ), F32),...  65.3 us
    pallas_call x1, Pallas kernels, shards(): pl.pallas_call(deliver, out_shape=tuple((jax.ShapeDtypeStruct(x.shape, F3...  1.4 us

profile of v5, /device:TPU:8, one launch (start us, length us, event | category | flops | bytes accessed | tf_op | source)
XLA Modules:
  0.0 67.3 jit_solution(11241185954041429950)
XLA Ops:
  0.6 65.3 %shard_map.148 = (f32[2048,128]{1,0:T(8,128)S(1)}, f32[2048,128]{1,0:T(8,128)S(1)}, f32[3,128,128]{2,1,0:T(8,128)S(1)}) custom-call(s32[16]{0:T(128)} %azimuth_hbm.1, s32[16]{0:T(128)} %radius_hbm.1, f32[1025]{0:T(1024)} %impedance_hbm.1, f32[2048,128]{1,0:T(8,128)} %bitcast.5, f32[2048,128]{1,0:T(8,128)} %bitcast.6, f32[2048,128]{1,0:T(8,128)} %bitcast.7, ...), custom_call_target="tpu_custom_call" | custom-call | tf_op jit(solution)/shard_map/pallas_call | solution.py:557
  65.9 1.4 %shard_map.149 = (f32[2048,128]{1,0:T(8,128)}, f32[2048,128]{1,0:T(8,128)}, f32[3,128,128]{2,1,0:T(8,128)}) custom-call(f32[2048,128]{1,0:T(8,128)S(1)} %get-tuple-element.9.dn, f32[2048,128]{1,0:T(8,128)S(1)} %get-tuple-element.10.press, f32[3,128,128]{2,1,0:T(8,128)S(1)} %get-tuple-element.11.acn), custom_call_target="tpu_custom_call" | custom-call | tf_op jit(solution)/shard_map/pallas_call | solution.py:614

commit v6 on v5

--- a/solution.py
+++ b/solution.py
@@ -387,7 +387,7 @@
             keep(row, pl.multiple_of(row + total * Q, 2 * Q), first_stage(x))
             return carry
 
-        lax.fori_loop(0, count // 2, pair, 0)
+        lax.fori_loop(0, count // 2, pair, 0, unroll=2)
         if extra:
             x = [jnp.concatenate([precv[n], precv[n]], 0) for n in range(SECTORS)]
             keep(offset + count * Q, offset + count * Q + total * Q, first_stage(x))
@@ -443,7 +443,7 @@
                         x2[place : place + 2 * Q, at] = part
             return carry
 
-        lax.fori_loop(0, NT // T, block, 0)
+        lax.fori_loop(0, NT // T, block, 0, unroll=2)
 
     def backward_chunk(c):
         start, count = RETURNS[c]

time: 67.4 us -> 67.2 us (level)
  no operation moved by 1% of the time
where the time goes in v6:
time: 67.2 us; the launch traced here: 67.1 us
  Pallas kernels  66.5 us (99%)
    pallas_call x1, Pallas kernels, shards(): pl.pallas_call(kernel, out_shape=(jax.ShapeDtypeStruct((T * R, NZ), F32),...  65.1 us
    pallas_call x1, Pallas kernels, shards(): pl.pallas_call(deliver, out_shape=tuple((jax.ShapeDtypeStruct(x.shape, F3...  1.4 us

profile of v6, /device:TPU:8, one launch (start us, length us, event | category | flops | bytes accessed | tf_op | source)
XLA Modules:
  0.0 67.1 jit_solution(8478207445416188915)
XLA Ops:
  0.6 65.1 %shard_map.148 = (f32[2048,128]{1,0:T(8,128)S(1)}, f32[2048,128]{1,0:T(8,128)S(1)}, f32[3,128,128]{2,1,0:T(8,128)S(1)}) custom-call(s32[16]{0:T(128)} %azimuth_hbm.1, s32[16]{0:T(128)} %radius_hbm.1, f32[1025]{0:T(1024)} %impedance_hbm.1, f32[2048,128]{1,0:T(8,128)} %bitcast.5, f32[2048,128]{1,0:T(8,128)} %bitcast.6, f32[2048,128]{1,0:T(8,128)} %bitcast.7, ...), custom_call_target="tpu_custom_call" | custom-call | tf_op jit(solution)/shard_map/pallas_call | solution.py:557
  65.7 1.4 %shard_map.149 = (f32[2048,128]{1,0:T(8,128)}, f32[2048,128]{1,0:T(8,128)}, f32[3,128,128]{2,1,0:T(8,128)}) custom-call(f32[2048,128]{1,0:T(8,128)S(1)} %get-tuple-element.9.dn, f32[2048,128]{1,0:T(8,128)S(1)} %get-tuple-element.10.press, f32[3,128,128]{2,1,0:T(8,128)S(1)} %get-tuple-element.11.acn), custom_call_target="tpu_custom_call" | custom-call | tf_op jit(solution)/shard_map/pallas_call | solution.py:614
